TPU v7x, 512 devices: a whole 4x4x16 slice. The times are simulated.
512 devices in a mesh: blk: 16 (over x, y_lo, core), bulk: 32 (over z, y_hi).
Axes of the slice: x: 4, y: 4 (y_hi: 2, y_lo: 2; y = y_hi * 2 + y_lo), z: 16, core: 2. Of those that a mesh axis runs over, the one named last changes fastest.
Arguments:
- targets: float32 [16, 128, 96, 192], P('blk', 'bulk'), may hold values from -1.5 to 1.5
- sources: float32 [16, 128, 96, 192], P('blk', 'bulk'), may hold values from -1.5 to 1.5
- permittivity: float32 [128, 96, 192], P('bulk'), may hold values from 2 to 4
Outputs:
- exchange_action: float32 [16, 128, 96, 192], P('blk', 'bulk')
All inputs are finite; a program needn't handle non-finite values.
Results may differ from a plain program's by a relative error of at most 0.0003.
Values sent between devices are 32-bit elements; how exact they have to be, the bound alone decides.
A program may use at most 64 MiB of HBM per device.

v0:
```python
import math

import jax
import jax.numpy as jnp
from jax import lax
from jax.sharding import PartitionSpec as P

SWEEPS = 3
CYCLE_STEPS = 2


source_scale = math.pi


def with_halo(cells, sides, width):
    for axis, dim in sides:
        count = lax.axis_size(axis)
        head = lax.slice_in_dim(cells, 0, width, axis=dim)
        tail = lax.slice_in_dim(cells, cells.shape[dim] - width, cells.shape[dim], axis=dim)
        cells = jnp.concatenate(
            [
                lax.ppermute(tail, axis, [(i, (i + 1) % count) for i in range(count)]),
                cells,
                lax.ppermute(head, axis, [((i + 1) % count, i) for i in range(count)]),
            ],
            axis=dim,
        )
    return cells


def passed_along(shard, axis, by):
    peers = lax.axis_size(axis)
    return lax.ppermute(shard, axis, [(i, (i + by) % peers) for i in range(peers)])


def coefficients(perm):
    ahead_x = 0.5 * (perm + jnp.roll(perm, -1, 1))
    ahead_y = 0.5 * (perm + jnp.roll(perm, -1, 2))
    faces_z = 0.5 * (perm[:-1] + perm[1:])
    behind_x = jnp.roll(ahead_x, 1, 1)[1:-1]
    behind_y = jnp.roll(ahead_y, 1, 2)[1:-1]
    ahead_x = ahead_x[1:-1]
    ahead_y = ahead_y[1:-1]
    ahead_z = faces_z[1:]
    behind_z = faces_z[:-1]
    diagonal = ahead_x + behind_x + ahead_y + behind_y + ahead_z + behind_z
    return (ahead_x, behind_x, ahead_y, behind_y, ahead_z, behind_z, diagonal)


def smooth(wider, rhs, coefs):
    ahead_x, behind_x, ahead_y, behind_y, ahead_z, behind_z, diagonal = coefs
    middle = wider[..., 1:-1, :, :]
    near = ahead_x * jnp.roll(middle, -1, -2) + behind_x * jnp.roll(middle, 1, -2)
    near = near + ahead_y * jnp.roll(middle, -1, -1) + behind_y * jnp.roll(middle, 1, -1)
    near = near + ahead_z * wider[..., 2:, :, :] + behind_z * wider[..., :-2, :, :]
    return (rhs + near) / diagonal


def shards(targets, sources, permittivity):
    perm_wide = with_halo(permittivity, (("bulk", 0),), 1)
    coefs = coefficients(perm_wide)
    visits = []
    current = sources
    for cycle_step in range(CYCLE_STEPS):
        current = passed_along(current, "blk", 1)
        visits.append(current)
    total = jnp.zeros(targets.shape, jnp.float32)
    for visit in visits:
        rhs = source_scale * (visit[:, None] * targets[None])
        potential = rhs / coefs[6]
        for sweep_index in range(SWEEPS):
            wider = with_halo(potential, (("bulk", 2),), 1)
            potential = smooth(wider, rhs, coefs)
        total = total + jnp.sum(visit[:, None] * potential, axis=0)
    return -total


def solution(mesh):
    in_specs = (P("blk", "bulk", None, None), P("blk", "bulk", None, None), P("bulk", None, None))
    out_specs = P("blk", "bulk", None, None)
    return jax.shard_map(shards, mesh=mesh, in_specs=in_specs, out_specs=out_specs, check_vma=False)
```

profile of v0, /device:TPU:32, one launch (start us, length us, event | category | flops | bytes accessed | tf_op | source)
XLA Modules:
  0.0 109.1 jit_solution(2298852181031867186)
XLA Ops:
  0.0 1.0 fusion.76
  1.0 5.1 %collective-permute-start.1 = (f32[1,96,192]{2,1,0:T(8,128)S(1)}, f32[1,96,192]{2,1,0:T(8,128)S(1)}, u32[]{:S(2)}, u32[]{:S(2)}) collective-permute-start(f32[1,96,192]{2,1,0:T(8,128)S(1)} %get-tuple-element.71), channel_id=1, source_target_pairs={{0,1},{1,2},{2,3},{3,4},{4,5},{5,6},{6,7},{7,8},{8,9},{9,10},{10,1... | collective-permute-start | bytes 221192 | tf_op jit(solution)/shard_map/ppermute | solution.py:22
  6.1 3.1 %collective-permute-start.2 = (f32[1,96,192]{2,1,0:T(8,128)S(1)}, f32[1,96,192]{2,1,0:T(8,128)S(1)}, u32[]{:S(2)}, u32[]{:S(2)}) collective-permute-start(f32[1,96,192]{2,1,0:T(8,128)S(1)} %get-tuple-element.70), channel_id=1, source_target_pairs={{1,0},{2,1},{3,2},{4,3},{5,4},{6,5},{7,6},{8,7},{9,8},{10,9},{11,1... | collective-permute-start | bytes 221192 | tf_op jit(solution)/shard_map/ppermute | solution.py:24
  9.3 1.9 %collective-permute-start = (f32[1,4,96,192]{3,2,1,0:T(8,128)}, f32[1,4,96,192]{3,2,1,0:T(8,128)S(1)}, u32[]{:S(2)}, u32[]{:S(2)}) collective-permute-start(f32[1,4,96,192]{3,2,1,0:T(8,128)} %param.4), channel_id=1, source_target_pairs={{0,32},{32,64},{64,96},{96,128},{128,160},{160,192},{192,224},{224... | collective-permute-start | bytes 884744 | tf_op jit(solution)/shard_map/ppermute | solution.py:33
  11.3 2.9 %collective-permute-done.2 = f32[1,96,192]{2,1,0:T(8,128)S(1)} collective-permute-done((f32[1,96,192]{2,1,0:T(8,128)S(1)}, f32[1,96,192]{2,1,0:T(8,128)S(1)}, u32[]{:S(2)}, u32[]{:S(2)}) %collective-permute-start.2) | collective-permute-done | bytes 73760 | tf_op jit(solution)/shard_map/ppermute | solution.py:24
  14.2 0.2 slice.389
  14.5 0.2 fusion
  14.7 0.1 slice.392
  14.9 5.8 %collective-permute-done = f32[1,4,96,192]{3,2,1,0:T(8,128)S(1)} collective-permute-done((f32[1,4,96,192]{3,2,1,0:T(8,128)}, f32[1,4,96,192]{3,2,1,0:T(8,128)S(1)}, u32[]{:S(2)}, u32[]{:S(2)}) %collective-permute-start) | collective-permute-done | bytes 294944 | tf_op jit(solution)/shard_map/ppermute | solution.py:33
  20.7 0.3 fusion.68
  21.0 0.1 slice_bitcast_fusion.34
  21.2 0.2 slice_bitcast_fusion.20
  21.3 5.9 %collective-permute-start.3 = (f32[1,1,1,96,192]{4,3,2,1,0:T(8,128)S(1)}, f32[1,1,1,96,192]{4,3,2,1,0:T(8,128)S(1)}, u32[]{:S(2)}, u32[]{:S(2)}) collective-permute-start(f32[1,1,1,96,192]{4,3,2,1,0:T(8,128)S(1)} %get-tuple-element.38), channel_id=1, source_target_pairs={{1,0},{2,1},{3,2},{4,3},{5,4},{6,5},{7,6},{8,7},{9,8},{10,9},{11,1... | collective-permute-start | bytes 221192 | tf_op jit(solution)/shard_map/ppermute | solution.py:24
  27.3 1.9 %collective-permute-start.4 = (f32[1,1,1,96,192]{4,3,2,1,0:T(8,128)S(1)}, f32[1,1,1,96,192]{4,3,2,1,0:T(8,128)S(1)}, u32[]{:S(2)}, u32[]{:S(2)}) collective-permute-start(f32[1,1,1,96,192]{4,3,2,1,0:T(8,128)S(1)} %get-tuple-element.39), channel_id=1, source_target_pairs={{0,1},{1,2},{2,3},{3,4},{4,5},{5,6},{6,7},{7,8},{8,9},{9,10},{10,1... | collective-permute-start | bytes 221192 | tf_op jit(solution)/shard_map/ppermute | solution.py:22
  29.2 1.9 %collective-permute-start.9 = (f32[1,4,96,192]{3,2,1,0:T(8,128)S(1)}, f32[1,4,96,192]{3,2,1,0:T(8,128)S(1)}, u32[]{:S(2)}, u32[]{:S(2)}) collective-permute-start(f32[1,4,96,192]{3,2,1,0:T(8,128)S(1)} %collective-permute-done), channel_id=1, source_target_pairs={{0,32},{32,64},{64,96},{96,128},{128,160},{160,192},{192,224},{224... | collective-permute-start | bytes 884744 | tf_op jit(solution)/shard_map/ppermute | solution.py:33
  31.2 8.4 %collective-permute-done.4 = f32[1,1,1,96,192]{4,3,2,1,0:T(8,128)S(1)} collective-permute-done((f32[1,1,1,96,192]{4,3,2,1,0:T(8,128)S(1)}, f32[1,1,1,96,192]{4,3,2,1,0:T(8,128)S(1)}, u32[]{:S(2)}, u32[]{:S(2)}) %collective-permute-start.4) | collective-permute-done | bytes 73760 | tf_op jit(solution)/shard_map/ppermute | solution.py:22
  39.6 0.6 fusion.39
  40.3 0.1 slice_bitcast_fusion.32
  40.4 0.2 slice_bitcast_fusion.16
  40.6 6.5 %collective-permute-start.5 = (f32[1,1,1,96,192]{4,3,2,1,0:T(8,128)S(1)}, f32[1,1,1,96,192]{4,3,2,1,0:T(8,128)S(1)}, u32[]{:S(2)}, u32[]{:S(2)}) collective-permute-start(f32[1,1,1,96,192]{4,3,2,1,0:T(8,128)S(1)} %get-tuple-element.28), channel_id=1, source_target_pairs={{1,0},{2,1},{3,2},{4,3},{5,4},{6,5},{7,6},{8,7},{9,8},{10,9},{11,1... | collective-permute-start | bytes 221192 | tf_op jit(solution)/shard_map/ppermute | solution.py:24
  47.1 1.9 %collective-permute-start.6 = (f32[1,1,1,96,192]{4,3,2,1,0:T(8,128)S(1)}, f32[1,1,1,96,192]{4,3,2,1,0:T(8,128)S(1)}, u32[]{:S(2)}, u32[]{:S(2)}) collective-permute-start(f32[1,1,1,96,192]{4,3,2,1,0:T(8,128)S(1)} %get-tuple-element.29), channel_id=1, source_target_pairs={{0,1},{1,2},{2,3},{3,4},{4,5},{5,6},{6,7},{7,8},{8,9},{9,10},{10,1... | collective-permute-start | bytes 221192 | tf_op jit(solution)/shard_map/ppermute | solution.py:22
  49.1 0.2 collective-permute-done.5
  49.3 6.7 %collective-permute-done.6 = f32[1,1,1,96,192]{4,3,2,1,0:T(8,128)S(1)} collective-permute-done((f32[1,1,1,96,192]{4,3,2,1,0:T(8,128)S(1)}, f32[1,1,1,96,192]{4,3,2,1,0:T(8,128)S(1)}, u32[]{:S(2)}, u32[]{:S(2)}) %collective-permute-start.6) | collective-permute-done | bytes 73760 | tf_op jit(solution)/shard_map/ppermute | solution.py:22
  56.0 0.6 fusion.33
  56.7 0.1 slice_bitcast_fusion.31
  56.8 0.2 slice_bitcast_fusion.13
  57.0 4.6 %collective-permute-start.7 = (f32[1,1,1,96,192]{4,3,2,1,0:T(8,128)S(1)}, f32[1,1,1,96,192]{4,3,2,1,0:T(8,128)S(1)}, u32[]{:S(2)}, u32[]{:S(2)}) collective-permute-start(f32[1,1,1,96,192]{4,3,2,1,0:T(8,128)S(1)} %get-tuple-element.18), channel_id=1, source_target_pairs={{1,0},{2,1},{3,2},{4,3},{5,4},{6,5},{7,6},{8,7},{9,8},{10,9},{11,1... | collective-permute-start | bytes 221192 | tf_op jit(solution)/shard_map/ppermute | solution.py:24
  61.7 2.7 %collective-permute-start.8 = (f32[1,1,1,96,192]{4,3,2,1,0:T(8,128)S(1)}, f32[1,1,1,96,192]{4,3,2,1,0:T(8,128)S(1)}, u32[]{:S(2)}, u32[]{:S(2)}) collective-permute-start(f32[1,1,1,96,192]{4,3,2,1,0:T(8,128)S(1)} %get-tuple-element.19), channel_id=1, source_target_pairs={{0,1},{1,2},{2,3},{3,4},{4,5},{5,6},{6,7},{7,8},{8,9},{9,10},{10,1... | collective-permute-start | bytes 221192 | tf_op jit(solution)/shard_map/ppermute | solution.py:22
  64.5 0.2 fusion.66
  64.9 0.2 slice_bitcast_fusion.8
  65.0 5.5 %collective-permute-start.10 = (f32[1,1,1,96,192]{4,3,2,1,0:T(8,128)S(1)}, f32[1,1,1,96,192]{4,3,2,1,0:T(8,128)S(1)}, u32[]{:S(2)}, u32[]{:S(2)}) collective-permute-start(f32[1,1,1,96,192]{4,3,2,1,0:T(8,128)S(1)} %get-tuple-element.68), channel_id=1, source_target_pairs={{1,0},{2,1},{3,2},{4,3},{5,4},{6,5},{7,6},{8,7},{9,8},{10,9},{11,1... | collective-permute-start | bytes 221192 | tf_op jit(solution)/shard_map/ppermute | solution.py:24
  70.6 1.9 %collective-permute-start.11 = (f32[1,1,1,96,192]{4,3,2,1,0:T(8,128)S(1)}, f32[1,1,1,96,192]{4,3,2,1,0:T(8,128)S(1)}, u32[]{:S(2)}, u32[]{:S(2)}) collective-permute-start(f32[1,1,1,96,192]{4,3,2,1,0:T(8,128)S(1)} %get-tuple-element.69), channel_id=1, source_target_pairs={{0,1},{1,2},{2,3},{3,4},{4,5},{5,6},{6,7},{7,8},{8,9},{9,10},{10,1... | collective-permute-start | bytes 221192 | tf_op jit(solution)/shard_map/ppermute | solution.py:22
  72.5 1.3 %collective-permute-done.10 = f32[1,1,1,96,192]{4,3,2,1,0:T(8,128)S(1)} collective-permute-done((f32[1,1,1,96,192]{4,3,2,1,0:T(8,128)S(1)}, f32[1,1,1,96,192]{4,3,2,1,0:T(8,128)S(1)}, u32[]{:S(2)}, u32[]{:S(2)}) %collective-permute-start.10) | collective-permute-done | bytes 73760 | tf_op jit(solution)/shard_map/ppermute | solution.py:24
  73.8 5.6 %collective-permute-done.11 = f32[1,1,1,96,192]{4,3,2,1,0:T(8,128)S(1)} collective-permute-done((f32[1,1,1,96,192]{4,3,2,1,0:T(8,128)S(1)}, f32[1,1,1,96,192]{4,3,2,1,0:T(8,128)S(1)}, u32[]{:S(2)}, u32[]{:S(2)}) %collective-permute-start.11) | collective-permute-done | bytes 73760 | tf_op jit(solution)/shard_map/ppermute | solution.py:22
  79.5 0.7 fusion.20
  80.4 0.2 slice_bitcast_fusion.4
  80.5 2.2 %collective-permute-start.12 = (f32[1,1,1,96,192]{4,3,2,1,0:T(8,128)S(1)}, f32[1,1,1,96,192]{4,3,2,1,0:T(8,128)S(1)}, u32[]{:S(2)}, u32[]{:S(2)}) collective-permute-start(f32[1,1,1,96,192]{4,3,2,1,0:T(8,128)S(1)} %get-tuple-element.58), channel_id=1, source_target_pairs={{1,0},{2,1},{3,2},{4,3},{5,4},{6,5},{7,6},{8,7},{9,8},{10,9},{11,1... | collective-permute-start | bytes 221192 | tf_op jit(solution)/shard_map/ppermute | solution.py:24
  82.8 5.1 %collective-permute-start.13 = (f32[1,1,1,96,192]{4,3,2,1,0:T(8,128)S(1)}, f32[1,1,1,96,192]{4,3,2,1,0:T(8,128)S(1)}, u32[]{:S(2)}, u32[]{:S(2)}) collective-permute-start(f32[1,1,1,96,192]{4,3,2,1,0:T(8,128)S(1)} %get-tuple-element.59), channel_id=1, source_target_pairs={{0,1},{1,2},{2,3},{3,4},{4,5},{5,6},{6,7},{7,8},{8,9},{9,10},{10,1... | collective-permute-start | bytes 221192 | tf_op jit(solution)/shard_map/ppermute | solution.py:22
  87.9 0.6 collective-permute-done.12
  88.5 3.5 %collective-permute-done.13 = f32[1,1,1,96,192]{4,3,2,1,0:T(8,128)S(1)} collective-permute-done((f32[1,1,1,96,192]{4,3,2,1,0:T(8,128)S(1)}, f32[1,1,1,96,192]{4,3,2,1,0:T(8,128)S(1)}, u32[]{:S(2)}, u32[]{:S(2)}) %collective-permute-start.13) | collective-permute-done | bytes 73760 | tf_op jit(solution)/shard_map/ppermute | solution.py:22
  92.0 0.6 fusion.14
  92.7 0.1 slice_bitcast_fusion.25
  92.8 0.2 slice_bitcast_fusion.1
  93.1 5.4 %collective-permute-start.14 = (f32[1,1,1,96,192]{4,3,2,1,0:T(8,128)S(1)}, f32[1,1,1,96,192]{4,3,2,1,0:T(8,128)S(1)}, u32[]{:S(2)}, u32[]{:S(2)}) collective-permute-start(f32[1,1,1,96,192]{4,3,2,1,0:T(8,128)S(1)} %get-tuple-element.48), channel_id=1, source_target_pairs={{1,0},{2,1},{3,2},{4,3},{5,4},{6,5},{7,6},{8,7},{9,8},{10,9},{11,1... | collective-permute-start | bytes 221192 | tf_op jit(solution)/shard_map/ppermute | solution.py:24
  98.5 1.9 %collective-permute-start.15 = (f32[1,1,1,96,192]{4,3,2,1,0:T(8,128)S(1)}, f32[1,1,1,96,192]{4,3,2,1,0:T(8,128)S(1)}, u32[]{:S(2)}, u32[]{:S(2)}) collective-permute-start(f32[1,1,1,96,192]{4,3,2,1,0:T(8,128)S(1)} %get-tuple-element.49), channel_id=1, source_target_pairs={{0,1},{1,2},{2,3},{3,4},{4,5},{5,6},{6,7},{7,8},{8,9},{9,10},{10,1... | collective-permute-start | bytes 221192 | tf_op jit(solution)/shard_map/ppermute | solution.py:22
  100.5 1.3 %collective-permute-done.14 = f32[1,1,1,96,192]{4,3,2,1,0:T(8,128)S(1)} collective-permute-done((f32[1,1,1,96,192]{4,3,2,1,0:T(8,128)S(1)}, f32[1,1,1,96,192]{4,3,2,1,0:T(8,128)S(1)}, u32[]{:S(2)}, u32[]{:S(2)}) %collective-permute-start.14) | collective-permute-done | bytes 73760 | tf_op jit(solution)/shard_map/ppermute | solution.py:24
  101.7 5.7 %collective-permute-done.15 = f32[1,1,1,96,192]{4,3,2,1,0:T(8,128)S(1)} collective-permute-done((f32[1,1,1,96,192]{4,3,2,1,0:T(8,128)S(1)}, f32[1,1,1,96,192]{4,3,2,1,0:T(8,128)S(1)}, u32[]{:S(2)}, u32[]{:S(2)}) %collective-permute-start.15) | collective-permute-done | bytes 73760 | tf_op jit(solution)/shard_map/ppermute | solution.py:22
  107.4 1.7 %negate_bitcast_fusion = f32[1,4,96,192]{3,2,1,0:T(8,128)} fusion(f32[1,1,4,96,192]{4,3,2,1,0:T(8,128)S(1)} %fusion.14, f32[1,1,1,96,192]{4,3,2,1,0:T(8,128)S(1)} %collective-permute-done.15, f32[1,1,1,96,192]{4,3,2,1,0:T(8,128)S(1)} %collective-permute-done.14, f32[4,96,192]{2,1,0:T(8,128)S(1)} %get-tuple-element.7, ...), kind=kLoop, calls=%fused_computation.139 | loop fusion | flops 3760128 | bytes 6193152 | tf_op jit(solution)/shard_map/neg | solution.py:75
  (37 shorter events, 0.9 us)
Async XLA Ops:
  0.0 11.2 %copy-start.1 = (f32[4,96,192]{2,1,0:T(8,128)S(1)}, f32[4,96,192]{2,1,0:T(8,128)}, u32[]{:S(2)}) copy-start(f32[4,96,192]{2,1,0:T(8,128)} %param.5) | copy-start | bytes 884740
  1.0 10.2 %collective-permute-start.1 = (f32[1,96,192]{2,1,0:T(8,128)S(1)}, f32[1,96,192]{2,1,0:T(8,128)S(1)}, u32[]{:S(2)}, u32[]{:S(2)}) collective-permute-start(f32[1,96,192]{2,1,0:T(8,128)S(1)} %get-tuple-element.71), channel_id=1, source_target_pairs={{0,1},{1,2},{2,3},{3,4},{4,5},{5,6},{6,7},{7,8},{8,9},{9,10},{10,1... | collective-permute-start | bytes 221192 | tf_op jit(solution)/shard_map/ppermute | solution.py:22
  6.1 8.0 %collective-permute-start.2 = (f32[1,96,192]{2,1,0:T(8,128)S(1)}, f32[1,96,192]{2,1,0:T(8,128)S(1)}, u32[]{:S(2)}, u32[]{:S(2)}) collective-permute-start(f32[1,96,192]{2,1,0:T(8,128)S(1)} %get-tuple-element.70), channel_id=1, source_target_pairs={{1,0},{2,1},{3,2},{4,3},{5,4},{6,5},{7,6},{8,7},{9,8},{10,9},{11,1... | collective-permute-start | bytes 221192 | tf_op jit(solution)/shard_map/ppermute | solution.py:24
  9.3 11.4 %collective-permute-start = (f32[1,4,96,192]{3,2,1,0:T(8,128)}, f32[1,4,96,192]{3,2,1,0:T(8,128)S(1)}, u32[]{:S(2)}, u32[]{:S(2)}) collective-permute-start(f32[1,4,96,192]{3,2,1,0:T(8,128)} %param.4), channel_id=1, source_target_pairs={{0,32},{32,64},{64,96},{96,128},{128,160},{160,192},{192,224},{224... | collective-permute-start | bytes 884744 | tf_op jit(solution)/shard_map/ppermute | solution.py:33
  14.8 5.9 %copy-start = (f32[1,4,96,192]{3,2,1,0:T(8,128)S(1)}, f32[1,4,96,192]{3,2,1,0:T(8,128)}, u32[]{:S(2)}) copy-start(f32[1,4,96,192]{3,2,1,0:T(8,128)} %param.3) | copy-start | bytes 884740
  21.3 9.8 %collective-permute-start.3 = (f32[1,1,1,96,192]{4,3,2,1,0:T(8,128)S(1)}, f32[1,1,1,96,192]{4,3,2,1,0:T(8,128)S(1)}, u32[]{:S(2)}, u32[]{:S(2)}) collective-permute-start(f32[1,1,1,96,192]{4,3,2,1,0:T(8,128)S(1)} %get-tuple-element.38), channel_id=1, source_target_pairs={{1,0},{2,1},{3,2},{4,3},{5,4},{6,5},{7,6},{8,7},{9,8},{10,9},{11,1... | collective-permute-start | bytes 221192 | tf_op jit(solution)/shard_map/ppermute | solution.py:24
  27.3 12.3 %collective-permute-start.4 = (f32[1,1,1,96,192]{4,3,2,1,0:T(8,128)S(1)}, f32[1,1,1,96,192]{4,3,2,1,0:T(8,128)S(1)}, u32[]{:S(2)}, u32[]{:S(2)}) collective-permute-start(f32[1,1,1,96,192]{4,3,2,1,0:T(8,128)S(1)} %get-tuple-element.39), channel_id=1, source_target_pairs={{0,1},{1,2},{2,3},{3,4},{4,5},{5,6},{6,7},{7,8},{8,9},{9,10},{10,1... | collective-permute-start | bytes 221192 | tf_op jit(solution)/shard_map/ppermute | solution.py:22
  29.2 35.2 %collective-permute-start.9 = (f32[1,4,96,192]{3,2,1,0:T(8,128)S(1)}, f32[1,4,96,192]{3,2,1,0:T(8,128)S(1)}, u32[]{:S(2)}, u32[]{:S(2)}) collective-permute-start(f32[1,4,96,192]{3,2,1,0:T(8,128)S(1)} %collective-permute-done), channel_id=1, source_target_pairs={{0,32},{32,64},{64,96},{96,128},{128,160},{160,192},{192,224},{224... | collective-permute-start | bytes 884744 | tf_op jit(solution)/shard_map/ppermute | solution.py:33
  40.6 8.7 %collective-permute-start.5 = (f32[1,1,1,96,192]{4,3,2,1,0:T(8,128)S(1)}, f32[1,1,1,96,192]{4,3,2,1,0:T(8,128)S(1)}, u32[]{:S(2)}, u32[]{:S(2)}) collective-permute-start(f32[1,1,1,96,192]{4,3,2,1,0:T(8,128)S(1)} %get-tuple-element.28), channel_id=1, source_target_pairs={{1,0},{2,1},{3,2},{4,3},{5,4},{6,5},{7,6},{8,7},{9,8},{10,9},{11,1... | collective-permute-start | bytes 221192 | tf_op jit(solution)/shard_map/ppermute | solution.py:24
  47.1 8.9 %collective-permute-start.6 = (f32[1,1,1,96,192]{4,3,2,1,0:T(8,128)S(1)}, f32[1,1,1,96,192]{4,3,2,1,0:T(8,128)S(1)}, u32[]{:S(2)}, u32[]{:S(2)}) collective-permute-start(f32[1,1,1,96,192]{4,3,2,1,0:T(8,128)S(1)} %get-tuple-element.29), channel_id=1, source_target_pairs={{0,1},{1,2},{2,3},{3,4},{4,5},{5,6},{6,7},{7,8},{8,9},{9,10},{10,1... | collective-permute-start | bytes 221192 | tf_op jit(solution)/shard_map/ppermute | solution.py:22
  57.0 43.4 %collective-permute-start.7 = (f32[1,1,1,96,192]{4,3,2,1,0:T(8,128)S(1)}, f32[1,1,1,96,192]{4,3,2,1,0:T(8,128)S(1)}, u32[]{:S(2)}, u32[]{:S(2)}) collective-permute-start(f32[1,1,1,96,192]{4,3,2,1,0:T(8,128)S(1)} %get-tuple-element.18), channel_id=1, source_target_pairs={{1,0},{2,1},{3,2},{4,3},{5,4},{6,5},{7,6},{8,7},{9,8},{10,9},{11,1... | collective-permute-start | bytes 221192 | tf_op jit(solution)/shard_map/ppermute | solution.py:24
  61.7 38.8 %collective-permute-start.8 = (f32[1,1,1,96,192]{4,3,2,1,0:T(8,128)S(1)}, f32[1,1,1,96,192]{4,3,2,1,0:T(8,128)S(1)}, u32[]{:S(2)}, u32[]{:S(2)}) collective-permute-start(f32[1,1,1,96,192]{4,3,2,1,0:T(8,128)S(1)} %get-tuple-element.19), channel_id=1, source_target_pairs={{0,1},{1,2},{2,3},{3,4},{4,5},{5,6},{6,7},{7,8},{8,9},{9,10},{10,1... | collective-permute-start | bytes 221192 | tf_op jit(solution)/shard_map/ppermute | solution.py:22
  65.0 8.8 %collective-permute-start.10 = (f32[1,1,1,96,192]{4,3,2,1,0:T(8,128)S(1)}, f32[1,1,1,96,192]{4,3,2,1,0:T(8,128)S(1)}, u32[]{:S(2)}, u32[]{:S(2)}) collective-permute-start(f32[1,1,1,96,192]{4,3,2,1,0:T(8,128)S(1)} %get-tuple-element.68), channel_id=1, source_target_pairs={{1,0},{2,1},{3,2},{4,3},{5,4},{6,5},{7,6},{8,7},{9,8},{10,9},{11,1... | collective-permute-start | bytes 221192 | tf_op jit(solution)/shard_map/ppermute | solution.py:24
  70.6 8.9 %collective-permute-start.11 = (f32[1,1,1,96,192]{4,3,2,1,0:T(8,128)S(1)}, f32[1,1,1,96,192]{4,3,2,1,0:T(8,128)S(1)}, u32[]{:S(2)}, u32[]{:S(2)}) collective-permute-start(f32[1,1,1,96,192]{4,3,2,1,0:T(8,128)S(1)} %get-tuple-element.69), channel_id=1, source_target_pairs={{0,1},{1,2},{2,3},{3,4},{4,5},{5,6},{6,7},{7,8},{8,9},{9,10},{10,1... | collective-permute-start | bytes 221192 | tf_op jit(solution)/shard_map/ppermute | solution.py:22
  80.5 8.0 %collective-permute-start.12 = (f32[1,1,1,96,192]{4,3,2,1,0:T(8,128)S(1)}, f32[1,1,1,96,192]{4,3,2,1,0:T(8,128)S(1)}, u32[]{:S(2)}, u32[]{:S(2)}) collective-permute-start(f32[1,1,1,96,192]{4,3,2,1,0:T(8,128)S(1)} %get-tuple-element.58), channel_id=1, source_target_pairs={{1,0},{2,1},{3,2},{4,3},{5,4},{6,5},{7,6},{8,7},{9,8},{10,9},{11,1... | collective-permute-start | bytes 221192 | tf_op jit(solution)/shard_map/ppermute | solution.py:24
  82.8 9.3 %collective-permute-start.13 = (f32[1,1,1,96,192]{4,3,2,1,0:T(8,128)S(1)}, f32[1,1,1,96,192]{4,3,2,1,0:T(8,128)S(1)}, u32[]{:S(2)}, u32[]{:S(2)}) collective-permute-start(f32[1,1,1,96,192]{4,3,2,1,0:T(8,128)S(1)} %get-tuple-element.59), channel_id=1, source_target_pairs={{0,1},{1,2},{2,3},{3,4},{4,5},{5,6},{6,7},{7,8},{8,9},{9,10},{10,1... | collective-permute-start | bytes 221192 | tf_op jit(solution)/shard_map/ppermute | solution.py:22
  93.1 8.7 %collective-permute-start.14 = (f32[1,1,1,96,192]{4,3,2,1,0:T(8,128)S(1)}, f32[1,1,1,96,192]{4,3,2,1,0:T(8,128)S(1)}, u32[]{:S(2)}, u32[]{:S(2)}) collective-permute-start(f32[1,1,1,96,192]{4,3,2,1,0:T(8,128)S(1)} %get-tuple-element.48), channel_id=1, source_target_pairs={{1,0},{2,1},{3,2},{4,3},{5,4},{6,5},{7,6},{8,7},{9,8},{10,9},{11,1... | collective-permute-start | bytes 221192 | tf_op jit(solution)/shard_map/ppermute | solution.py:24
  98.5 8.9 %collective-permute-start.15 = (f32[1,1,1,96,192]{4,3,2,1,0:T(8,128)S(1)}, f32[1,1,1,96,192]{4,3,2,1,0:T(8,128)S(1)}, u32[]{:S(2)}, u32[]{:S(2)}) collective-permute-start(f32[1,1,1,96,192]{4,3,2,1,0:T(8,128)S(1)} %get-tuple-element.49), channel_id=1, source_target_pairs={{0,1},{1,2},{2,3},{3,4},{4,5},{5,6},{6,7},{7,8},{8,9},{9,10},{10,1... | collective-permute-start | bytes 221192 | tf_op jit(solution)/shard_map/ppermute | solution.py:22
where the time goes:
time: 110 us; the launch traced here: 109 us
  starting transfers between devices  57.8 us (53%)
  waiting for transfers between devices  42.1 us (38%)
  other arithmetic  5.01 us (5%)
  local copies, waits for them, and re-layouts  3.76 us (3%)
    ppermute x7, starting transfers between devices, with_halo(): lax.ppermute(head, axis, [((i + 1) % count, i) for i in range(count)])  33.4 us
    ppermute x7, waiting for transfers between devices, with_halo(): lax.ppermute(tail, axis, [(i, (i + 1) % count) for i in range(count)])  29.9 us
    ppermute x7, starting transfers between devices, with_halo(): lax.ppermute(tail, axis, [(i, (i + 1) % count) for i in range(count)])  20.6 us
    ppermute x7, waiting for transfers between devices, with_halo(): lax.ppermute(head, axis, [((i + 1) % count, i) for i in range(count)])  6.35 us
    ppermute x2, waiting for transfers between devices, passed_along(): lax.ppermute(shard, axis, [(i, (i + by) % peers) for i in range(peers)])  5.81 us
    ppermute x2, starting transfers between devices, passed_along(): lax.ppermute(shard, axis, [(i, (i + by) % peers) for i in range(peers)])  3.84 us
    div x4, other arithmetic, smooth(): return (rhs + near) / diagonal  2.59 us
  transfers between devices with their start and end apart: 16, of which 11 were waited for; matrix products, arithmetic and copies ran while one was open for 5% of the time, Pallas kernels for 0%

commit v1 on v0

v1 whole, which is shorter than its diff:
```python
import functools
import math

import jax
import jax.numpy as jnp
from jax import lax
from jax.experimental import pallas as pl
from jax.experimental.pallas import tpu as pltpu
from jax.sharding import PartitionSpec as P

MESH = pl.DeviceIdType.MESH
SLAB = 4
WIDE = 256
SCALE = math.pi


def packed(plane):
    lines = plane.shape[0]
    right = plane[:, 128:192]
    return plane[:, 0:128], jnp.concatenate([right[: lines // 2], right[lines // 2 :]], axis=1)


def unpacked(both):
    lines = both.shape[0] * 2 // 3
    left, right = both[:lines], both[lines:]
    left_turned = pltpu.roll(left, 64, 1)
    right_turned = pltpu.roll(right, 64, 1)
    lane = lax.broadcasted_iota(jnp.int32, right.shape, 1)
    low = jnp.where(lane < 64, right, jnp.where(lane < 96, left_turned[: lines // 2], right_turned))
    high = jnp.where(lane < 64, right_turned, jnp.where(lane < 96, left_turned[lines // 2 :], right))
    return left, jnp.concatenate([low, high], axis=0)


def ahead(cells, axis):
    return pltpu.roll(cells, cells.shape[axis] - 1, axis)


def behind(cells, axis):
    return pltpu.roll(cells, 1, axis)


def kernel(
    n_blk, n_bulk,
    t_hbm, s_hbm, e_hbm, out_ref,
    t_in, s_in, e_in, own_s, tgt, direct, passed, eps, eps_wide, coef, inverse, first, mid, late,
    in_sem, send_sem, recv_sem,
):
    b, k = lax.axis_index("blk"), lax.axis_index("bulk")
    core, lo, hi = lax.rem(b, 2), lax.rem(b // 2, 2), lax.rem(k, 2)
    lines = t_in.shape[1]
    other_k = k + 1 - 2 * hi
    next_b, prev_b = lax.rem(b + 2, n_blk), lax.rem(b + n_blk - 2, n_blk)
    partner = (b, other_k)
    chip_mate = (b + 1 - 2 * core, k)
    next_same, next_other = (next_b, k), (next_b, other_k)
    prev_same, prev_other = (prev_b, k), (prev_b, other_k)
    beside = (b + 2 - 4 * lo, other_k)
    z_to = (b, lax.rem(k + n_bulk + 2 - 4 * hi, n_bulk))
    z_from = (b, lax.rem(k + n_bulk - 2 + 4 * hi, n_bulk))

    loads = [
        pltpu.make_async_copy(src, dst, in_sem.at[i])
        for i, (src, dst) in enumerate(((s_hbm.at[0], s_in), (t_hbm.at[0], t_in), (e_hbm, e_in)))
    ]
    for load in loads:
        load.start()

    barrier = pltpu.get_barrier_semaphore()

    def tell(devices):
        for device in devices:
            pl.semaphore_signal(barrier, inc=1, device_id=device, device_id_type=MESH)

    tell((partner, prev_same, prev_other, z_from, chip_mate))

    @pl.when(core == 0)
    def _():
        tell((beside,))

    own = 3 + hi
    far = 7 * (1 - hi)
    far_there = 7 * hi
    z_src, z_dst = 8 * (1 - hi), 8 * hi

    def pack(src, dst, at):
        def body(i, _):
            left, right = packed(src[i])
            dst[at + i, 0:lines] = left
            dst[at + i, lines:] = right
            return 0
        lax.fori_loop(0, SLAB, body, 0)

    loads[0].wait()
    pack(s_in, own_s, 0)
    loads[1].wait()
    pack(t_in, tgt, own)
    loads[2].wait()
    pack(e_in, eps, 4)

    @pl.when(core == 0)
    def _():
        pl.semaphore_wait(barrier, 6)

    @pl.when(core == 1)
    def _():
        pl.semaphore_wait(barrier, 5)

    def copy(i, src, src_at, dst, dst_at, count, device):
        return pltpu.make_async_remote_copy(
            src_ref=src.at[pl.ds(src_at, count)], dst_ref=dst.at[pl.ds(dst_at, count)],
            send_sem=send_sem.at[i], recv_sem=recv_sem.at[i], device_id=device, device_id_type=MESH,
        )

    tgt_far = copy(0, tgt, own, tgt, far_there, 4, partner)
    tgt_z = copy(1, tgt, z_src, tgt, z_dst, 3, z_to)
    direct_own = copy(2, own_s, 0, direct, own, 4, next_same)
    direct_far = copy(3, own_s, 0, direct, far_there, 4, next_other)
    direct_z = copy(4, direct, z_src, direct, z_dst, 3, z_to)
    eps_far = copy(5, eps, 4, eps, 8 * hi, 4, beside)
    eps_z = copy(6, eps, z_src, eps, z_dst, 4, z_to)
    mate_own_s = copy(7, own_s, 0, passed, own, 4, chip_mate)
    mate_eps_far = copy(8, eps, z_src, eps, z_src, 4, chip_mate)
    mate_eps_z = copy(9, eps, z_dst, eps, z_dst, 4, chip_mate)
    passed_far = copy(10, passed, own, passed, far_there, 4, partner)
    passed_z = copy(11, passed, z_src, passed, z_dst, 3, z_to)
    mate_direct_own = copy(7, direct, own, passed, own, 4, chip_mate)
    mate_direct_far = copy(8, direct, far, passed, far, 4, chip_mate)
    mate_direct_z = copy(9, direct, z_dst, passed, z_dst, 3, chip_mate)

    @pl.when(core == 0)
    def _():
        mate_own_s.start()
        eps_far.start()
        tgt_far.start()
        direct_far.start()
        direct_own.start()
        eps_far.wait_recv()
        eps_z.start()
        mate_eps_far.start()
        tgt_far.wait_recv()
        tgt_z.start()
        direct_far.wait_recv()
        direct_z.start()
        eps_z.wait_recv()
        mate_eps_z.start()

    @pl.when(core == 1)
    def _():
        tgt_far.start()
        direct_far.start()
        mate_own_s.wait_recv()
        passed_far.start()
        direct_own.start()
        tgt_far.wait_recv()
        tgt_z.start()
        direct_far.wait_recv()
        direct_z.start()
        mate_direct_far.start()
        passed_far.wait_recv()
        passed_z.start()
        direct_own.wait_recv()
        mate_direct_own.start()
        direct_z.wait_recv()
        mate_direct_z.start()
        mate_eps_far.wait_recv()
        mate_eps_z.wait_recv()

    def wide_body(i, _):
        left, right = unpacked(eps[i])
        eps_wide[i, :, 0:128] = left
        eps_wide[i, :, 128:WIDE] = right
        return 0

    lax.fori_loop(0, 12, wide_body, 0)

    def coef_body(i, _):
        cells = eps_wide[i + 1]
        ahead_x = 0.5 * (cells + ahead(cells, 0))
        ahead_y = 0.5 * (cells + ahead(cells, 1))
        ahead_z = 0.5 * (cells + eps_wide[i + 2])
        behind_x = behind(ahead_x, 0)
        behind_y = behind(ahead_y, 1)
        behind_z = 0.5 * (cells + eps_wide[i])
        inv = 1.0 / (ahead_x + behind_x + ahead_y + behind_y + ahead_z + behind_z)
        inverse[i] = SCALE * inv
        for j, face in enumerate((ahead_x, behind_x, ahead_y, behind_y, ahead_z, behind_z)):
            coef[j, i] = face * inv
        return 0

    lax.fori_loop(0, 10, coef_body, 0)

    def swept(src, i, start):
        cells = src[i]
        near = first[start] + coef[0, start] * ahead(cells, 0) + coef[1, start] * behind(cells, 0)
        near = near + coef[2, start] * ahead(cells, 1) + coef[3, start] * behind(cells, 1)
        return near + coef[4, start] * src[i + 1] + coef[5, start] * src[i - 1]

    def pair(source, add):
        def first_body(i, _):
            left, right = unpacked(source[i + hi] * tgt[i + hi])
            first[i, :, 0:128] = left * inverse[i, :, 0:128]
            first[i, :, 128:WIDE] = right * inverse[i, :, 128:WIDE]
            return 0

        lax.fori_loop(0, 10, first_body, 0)

        def mid_body(i, _):
            mid[i] = swept(first, i + 1, i + 1)
            return 0

        lax.fori_loop(0, 8, mid_body, 0)

        def late_body(i, _):
            late[i] = swept(mid, i + 1, i + 2)
            return 0

        lax.fori_loop(0, 6, late_body, 0)

        def out_body(i, _):
            potential = swept(late, i + 1, i + 3)
            left, right = unpacked(source[own + i])
            left = left * potential[:, 0:128]
            right = right[:, 0:64] * potential[:, 128:192]
            if add:
                out_ref[0, i, :, 0:128] = out_ref[0, i, :, 0:128] - left
                out_ref[0, i, :, 128:192] = out_ref[0, i, :, 128:192] - right
            else:
                out_ref[0, i, :, 0:128] = -left
                out_ref[0, i, :, 128:192] = -right
            return 0

        lax.fori_loop(0, SLAB, out_body, 0)

    tgt_z.wait_recv()

    @pl.when(core == 0)
    def _():
        direct_own.wait_recv()
        direct_z.wait_recv()

    pair(direct, False)

    @pl.when(core == 0)
    def _():
        mate_direct_own.wait_recv()
        mate_direct_far.wait_recv()
        mate_direct_z.wait_recv()

    @pl.when(core == 1)
    def _():
        passed_z.wait_recv()

    pair(passed, True)

    for sent in (tgt_far, tgt_z, direct_own, direct_far, direct_z):
        sent.wait_send()

    @pl.when(core == 0)
    def _():
        for sent in (eps_far, eps_z, mate_own_s, mate_eps_far, mate_eps_z):
            sent.wait_send()

    @pl.when(core == 1)
    def _():
        for sent in (passed_far, passed_z, mate_direct_own, mate_direct_far, mate_direct_z):
            sent.wait_send()


def shards(n_blk, n_bulk, targets, sources, permittivity):
    _, planes, lines, cells = targets.shape
    rows = lines * cells // 128

    def plane_stack(count, *tile):
        return pltpu.VMEM((count, *tile), jnp.float32)

    return pl.pallas_call(
        functools.partial(kernel, n_blk, n_bulk),
        out_shape=jax.ShapeDtypeStruct(targets.shape, jnp.float32),
        in_specs=[pl.BlockSpec(memory_space=pl.ANY)] * 3,
        out_specs=pl.BlockSpec(memory_space=pltpu.VMEM),
        scratch_shapes=[
            plane_stack(planes, lines, cells),
            plane_stack(planes, lines, cells),
            plane_stack(planes, lines, cells),
            plane_stack(planes, rows, 128),
            plane_stack(11, rows, 128),
            plane_stack(11, rows, 128),
            plane_stack(11, rows, 128),
            plane_stack(12, rows, 128),
            plane_stack(12, lines, WIDE),
            pltpu.VMEM((6, 10, lines, WIDE), jnp.float32),
            plane_stack(10, lines, WIDE),
            plane_stack(10, lines, WIDE),
            plane_stack(8, lines, WIDE),
            plane_stack(6, lines, WIDE),
            pltpu.SemaphoreType.DMA((3,)),
            pltpu.SemaphoreType.DMA((12,)),
            pltpu.SemaphoreType.DMA((12,)),
        ],
        compiler_params=pltpu.CompilerParams(collective_id=0, has_side_effects=True, vmem_limit_bytes=40 << 20),
        cost_estimate=pl.CostEstimate(flops=20_000_000, bytes_accessed=1_200_000, transcendentals=0),
    )(targets, sources, permittivity)


def solution(mesh):
    in_specs = (P("blk", "bulk", None, None), P("blk", "bulk", None, None), P("bulk", None, None))
    out_specs = P("blk", "bulk", None, None)
    return jax.shard_map(
        functools.partial(shards, mesh.shape["blk"], mesh.shape["bulk"]),
        mesh=mesh, in_specs=in_specs, out_specs=out_specs, check_vma=False,
    )
```

time: 110 us -> 56.9 us (0.52)
  the two profiles are of different devices: /device:TPU:32 before, /device:TPU:1 now
where the time goes in v1:
time: 56.9 us; the launch traced here: 56.7 us
  Pallas kernels  52.9 us (93%)
  local copies, waits for them, and re-layouts  3.73 us (7%)
    pallas_call x1, Pallas kernels, shards(): pl.pallas_call(functools.partial(kernel, n_blk, n_bulk), out_shape=jax.Sh...  52.9 us
    unnamed x7, local copies, waits for them, and re-layouts  3.73 us

profile of v1, /device:TPU:1, one launch (start us, length us, event | category | flops | bytes accessed | tf_op | source)
XLA Modules:
  0.0 56.7 jit_solution(15755304611222808875)
XLA Ops:
  0.0 0.0 copy-start
  0.0 1.0 %copy-done = f32[1,4,96,192]{3,2,1,0:T(8,128)S(1)} copy-done((f32[1,4,96,192]{3,2,1,0:T(8,128)S(1)}, f32[1,4,96,192]{3,2,1,0:T(8,128)}, u32[]{:S(2)}) %copy-start) | copy-done | bytes 294936
  1.0 0.0 copy-start.1
  1.0 1.0 %copy-done.1 = f32[1,4,96,192]{3,2,1,0:T(8,128)S(1)} copy-done((f32[1,4,96,192]{3,2,1,0:T(8,128)S(1)}, f32[1,4,96,192]{3,2,1,0:T(8,128)}, u32[]{:S(2)}) %copy-start.1) | copy-done | bytes 294936
  2.0 0.0 copy-start.2
  2.0 1.0 %copy-done.2 = f32[4,96,192]{2,1,0:T(8,128)S(1)} copy-done((f32[4,96,192]{2,1,0:T(8,128)S(1)}, f32[4,96,192]{2,1,0:T(8,128)}, u32[]{:S(2)}) %copy-start.2) | copy-done | bytes 294936
  3.0 52.9 %shard_map.37 = f32[1,4,96,192]{3,2,1,0:T(8,128)S(1)} custom-call(f32[1,4,96,192]{3,2,1,0:T(8,128)S(1)} %copy-done, f32[1,4,96,192]{3,2,1,0:T(8,128)S(1)} %copy-done.1, f32[4,96,192]{2,1,0:T(8,128)S(1)} %copy-done.2), custom_call_target="tpu_custom_call" | custom-call | flops 20000000 | bytes 1200000 | tf_op jit(solution)/shard_map/pallas_call | solution.py:276
  55.9 0.7 %copy.5 = f32[1,4,96,192]{3,2,1,0:T(8,128)} copy(f32[1,4,96,192]{3,2,1,0:T(8,128)S(1)} %shard_map.37) | data formatting | bytes 589824
Async XLA Ops:
  0.0 1.0 %copy-start = (f32[1,4,96,192]{3,2,1,0:T(8,128)S(1)}, f32[1,4,96,192]{3,2,1,0:T(8,128)}, u32[]{:S(2)}) copy-start(f32[1,4,96,192]{3,2,1,0:T(8,128)} %t_hbm.1) | copy-start | bytes 884740
  1.0 1.0 %copy-start.1 = (f32[1,4,96,192]{3,2,1,0:T(8,128)S(1)}, f32[1,4,96,192]{3,2,1,0:T(8,128)}, u32[]{:S(2)}) copy-start(f32[1,4,96,192]{3,2,1,0:T(8,128)} %s_hbm.1) | copy-start | bytes 884740
  2.0 1.0 %copy-start.2 = (f32[4,96,192]{2,1,0:T(8,128)S(1)}, f32[4,96,192]{2,1,0:T(8,128)}, u32[]{:S(2)}) copy-start(f32[4,96,192]{2,1,0:T(8,128)} %e_hbm.1) | copy-start | bytes 884740

commit v2 on v1

v2 whole, which is shorter than its diff:
```python
import functools
import math

import jax
import jax.numpy as jnp
from jax import lax
from jax.experimental import pallas as pl
from jax.experimental.pallas import tpu as pltpu
from jax.sharding import PartitionSpec as P

MESH = pl.DeviceIdType.MESH
SLAB = 4
WIDE = 256
SCALE = math.pi


def packed(plane):
    lines = plane.shape[0]
    right = plane[:, 128:192]
    return plane[:, 0:128], jnp.concatenate([right[: lines // 2], right[lines // 2 :]], axis=1)


def unpacked(both):
    lines = both.shape[0] * 2 // 3
    left, right = both[:lines], both[lines:]
    left_turned = pltpu.roll(left, 64, 1)
    right_turned = pltpu.roll(right, 64, 1)
    lane = lax.broadcasted_iota(jnp.int32, right.shape, 1)
    low = jnp.where(lane < 64, right, jnp.where(lane < 96, left_turned[: lines // 2], right_turned))
    high = jnp.where(lane < 64, right_turned, jnp.where(lane < 96, left_turned[lines // 2 :], right))
    return left, jnp.concatenate([low, high], axis=0)


def ahead(cells, axis):
    return pltpu.roll(cells, cells.shape[axis] - 1, axis)


def behind(cells, axis):
    return pltpu.roll(cells, 1, axis)


def kernel(
    n_blk, n_bulk,
    t_hbm, s_hbm, e_hbm, out_ref,
    t_in, s_in, e_in, own_s, own_t, tgt, near_s, next_s, eps, done, back, eps_wide, coef, inverse, first, mid, late, total,
    in_sem, send_sem, recv_sem,
):
    b, k = lax.axis_index("blk"), lax.axis_index("bulk")
    pos, core, z, hi = b // 2, lax.rem(b, 2), k // 2, lax.rem(k, 2)
    n_pos = n_blk // 2
    lines = t_in.shape[1]
    home = core == hi
    away = core != hi
    prev_pos, next_pos = lax.rem(pos + n_pos - 1, n_pos), lax.rem(pos + 1, n_pos)
    mate = (b + 1 - 2 * core, k)
    beyond = (b + 1 - 2 * core, lax.rem(k + n_bulk - 2 + 4 * core, n_bulk))
    swap = (b + 1 - 2 * core, k + 1 - 2 * hi)
    beside = (b + 2 - 4 * lax.rem(pos, 2), k + 1 - 2 * hi)
    to_one = (lax.rem(pos + core, n_pos) * 2 + hi, 2 * z + 1 - core)
    to_two = (next_pos * 2 + hi, 2 * z + core)
    from_one = (lax.rem(pos + n_pos - 1 + hi, n_pos) * 2 + 1 - hi, 2 * z + core)
    from_two = (prev_pos * 2 + hi, 2 * z + core)

    loads = [
        pltpu.make_async_copy(src, dst, in_sem.at[i])
        for i, (src, dst) in enumerate(((s_hbm.at[0], s_in), (t_hbm.at[0], t_in), (e_hbm, e_in)))
    ]
    for load in loads:
        load.start()

    barrier = pltpu.get_barrier_semaphore()

    def tell(devices):
        for device in devices:
            pl.semaphore_signal(barrier, inc=1, device_id=device, device_id_type=MESH)

    tell((from_one, from_two, mate, beyond))

    @pl.when(away)
    def _():
        tell((swap, beside))

    def pack(src, dst, at):
        def body(i, _):
            left, right = packed(src[i])
            dst[at + i, 0:lines] = left
            dst[at + i, lines:] = right
            return 0
        lax.fori_loop(0, SLAB, body, 0)

    def copy(i, src, src_at, dst, dst_at, count, device):
        return pltpu.make_async_remote_copy(
            src_ref=src.at[pl.ds(src_at, count)], dst_ref=dst.at[pl.ds(dst_at, count)],
            send_sem=send_sem.at[i], recv_sem=recv_sem.at[i], device_id=device, device_id_type=MESH,
        )

    def relays(i, buf):
        return (
            copy(i, buf, 4 - core, buf, 7 * core, 3, mate),
            copy(i + 1, buf, 3 + core, buf, 7 * (1 - core), 3, beyond),
        )

    source_one = copy(0, own_s, 0, near_s, 3, SLAB, to_one)
    source_two = copy(1, own_s, 0, next_s, 3, SLAB, to_two)
    target = copy(2, own_t, 0, tgt, 3, SLAB, swap)
    perm = copy(3, eps, 4, eps, 4, SLAB, beside)
    tgt_mate, tgt_beyond = relays(4, tgt)
    near_mate, near_beyond = relays(6, near_s)
    next_mate, next_beyond = relays(8, next_s)
    eps_mate = copy(10, eps, 4, eps, 8 * core, SLAB, mate)
    eps_beyond = copy(11, eps, 4, eps, 8 * (1 - core), SLAB, beyond)

    def result(i):
        return copy(12 + i, done, i, back, i, 1, swap)

    loads[0].wait()
    pack(s_in, own_s, 0)
    loads[1].wait()
    loads[2].wait()

    @pl.when(away)
    def _():
        pack(t_in, own_t, 0)

    @pl.when(home)
    def _():
        pack(t_in, tgt, 3)
        pack(e_in, eps, 4)

    pl.semaphore_wait(barrier, 5)

    def wide_body(i, _):
        left, right = unpacked(eps[i])
        eps_wide[i, :, 0:128] = left
        eps_wide[i, :, 128:WIDE] = right
        return 0

    def coef_body(i, _):
        cells = eps_wide[i + 1]
        ahead_x = 0.5 * (cells + ahead(cells, 0))
        ahead_y = 0.5 * (cells + ahead(cells, 1))
        ahead_z = 0.5 * (cells + eps_wide[i + 2])
        behind_x = behind(ahead_x, 0)
        behind_y = behind(ahead_y, 1)
        behind_z = 0.5 * (cells + eps_wide[i])
        inv = 1.0 / (ahead_x + behind_x + ahead_y + behind_y + ahead_z + behind_z)
        inverse[i] = SCALE * inv
        for j, face in enumerate((ahead_x, behind_x, ahead_y, behind_y, ahead_z, behind_z)):
            coef[j, i] = face * inv
        return 0

    @pl.when(home)
    def _():
        source_one.start()
        perm.start()
        source_two.start()
        eps_mate.start()
        eps_beyond.start()
        tgt_mate.start()
        tgt_beyond.start()

    @pl.when(away)
    def _():
        target.start()
        source_one.start()
        source_two.start()
        perm.wait_recv()
        eps_mate.start()
        eps_beyond.start()
        target.wait_recv()
        tgt_mate.start()
        tgt_beyond.start()

    source_one.wait_recv()
    near_mate.start()
    near_beyond.start()

    eps_mate.wait_recv()
    eps_beyond.wait_recv()
    lax.fori_loop(0, 12, wide_body, 0)
    lax.fori_loop(0, 10, coef_body, 0)

    source_two.wait_recv()
    next_mate.start()
    next_beyond.start()

    def swept(src, i, start):
        cells = src[i]
        near = first[start] + coef[0, start] * ahead(cells, 0) + coef[1, start] * behind(cells, 0)
        near = near + coef[2, start] * ahead(cells, 1) + coef[3, start] * behind(cells, 1)
        return near + coef[4, start] * src[i + 1] + coef[5, start] * src[i - 1]

    def pair(source, last):
        def first_body(i, _):
            left, right = unpacked(source[i] * tgt[i])
            first[i, :, 0:128] = left * inverse[i, :, 0:128]
            first[i, :, 128:WIDE] = right * inverse[i, :, 128:WIDE]
            return 0

        lax.fori_loop(0, 10, first_body, 0)

        def mid_body(i, _):
            mid[i] = swept(first, i + 1, i + 1)
            return 0

        lax.fori_loop(0, 8, mid_body, 0)

        def late_body(i, _):
            late[i] = swept(mid, i + 1, i + 2)
            return 0

        lax.fori_loop(0, 6, late_body, 0)

        def out_body(i, _):
            potential = swept(late, i + 1, i + 3)
            left, right = unpacked(source[3 + i])
            left = left * potential[:, 0:128]
            right = right * potential[:, 128:WIDE]
            if not last:
                total[i, :, 0:128] = left
                total[i, :, 128:WIDE] = right
                return 0
            left = -(total[i, :, 0:128] + left)
            right = -(total[i, :, 128:WIDE] + right)

            @pl.when(home)
            def _():
                out_ref[0, i, :, 0:128] = left
                out_ref[0, i, :, 128:192] = right[:, 0:64]

            @pl.when(away)
            def _():
                done[i, 0:lines] = left
                done[i, lines:] = jnp.concatenate([right[: lines // 2, 0:64], right[lines // 2 :, 0:64]], axis=1)
                result(i).start()
            return 0

        lax.fori_loop(0, SLAB, out_body, 0)

    tgt_mate.wait_recv()
    tgt_beyond.wait_recv()
    near_mate.wait_recv()
    near_beyond.wait_recv()
    pair(near_s, False)
    next_mate.wait_recv()
    next_beyond.wait_recv()
    pair(next_s, True)

    for sent in (source_one, source_two, tgt_mate, tgt_beyond, near_mate, near_beyond, next_mate, next_beyond, eps_mate, eps_beyond):
        sent.wait_send()

    @pl.when(home)
    def _():
        perm.wait_send()

    @pl.when(away)
    def _():
        target.wait_send()

        def back_body(i, _):
            result(i).wait()
            left, right = unpacked(back[i])
            out_ref[0, i, :, 0:128] = left
            out_ref[0, i, :, 128:192] = right[:, 0:64]
            return 0

        lax.fori_loop(0, SLAB, back_body, 0)


def shards(n_blk, n_bulk, targets, sources, permittivity):
    _, planes, lines, cells = targets.shape
    rows = lines * cells // 128

    def plane_stack(count, *tile):
        return pltpu.VMEM((count, *tile), jnp.float32)

    return pl.pallas_call(
        functools.partial(kernel, n_blk, n_bulk),
        out_shape=jax.ShapeDtypeStruct(targets.shape, jnp.float32),
        in_specs=[pl.BlockSpec(memory_space=pl.ANY)] * 3,
        out_specs=pl.BlockSpec(memory_space=pltpu.VMEM),
        scratch_shapes=[
            plane_stack(planes, lines, cells),
            plane_stack(planes, lines, cells),
            plane_stack(planes, lines, cells),
            plane_stack(planes, rows, 128),
            plane_stack(planes, rows, 128),
            plane_stack(10, rows, 128),
            plane_stack(10, rows, 128),
            plane_stack(10, rows, 128),
            plane_stack(12, rows, 128),
            plane_stack(planes, rows, 128),
            plane_stack(planes, rows, 128),
            plane_stack(12, lines, WIDE),
            pltpu.VMEM((6, 10, lines, WIDE), jnp.float32),
            plane_stack(10, lines, WIDE),
            plane_stack(10, lines, WIDE),
            plane_stack(8, lines, WIDE),
            plane_stack(6, lines, WIDE),
            plane_stack(planes, lines, WIDE),
            pltpu.SemaphoreType.DMA((3,)),
            pltpu.SemaphoreType.DMA((16,)),
            pltpu.SemaphoreType.DMA((16,)),
        ],
        compiler_params=pltpu.CompilerParams(collective_id=0, has_side_effects=True, vmem_limit_bytes=60 << 20),
        cost_estimate=pl.CostEstimate(flops=20_000_000, bytes_accessed=1_200_000, transcendentals=0),
    )(targets, sources, permittivity)


def solution(mesh):
    in_specs = (P("blk", "bulk", None, None), P("blk", "bulk", None, None), P("bulk", None, None))
    out_specs = P("blk", "bulk", None, None)
    return jax.shard_map(
        functools.partial(shards, mesh.shape["blk"], mesh.shape["bulk"]),
        mesh=mesh, in_specs=in_specs, out_specs=out_specs, check_vma=False,
    )
```

time: 56.9 us -> 50.2 us (0.88)
  Pallas kernels: 52.9 us -> 48.3 us
  local copies, waits for them, and re-layouts: 3.73 us -> 1.77 us
    pallas_call x1, Pallas kernels: 52.9 us -> 48.3 us  [shards(): pl.pallas_call(functools.partial(kernel, n_blk, n_bulk), out_shape=jax.Sh...]
    unnamed x7 -> x1, local copies, waits for them, and re-layouts: 3.73 us -> 1.77 us
where the time goes in v2:
time: 50.2 us; the launch traced here: 50.1 us
  Pallas kernels  48.3 us (96%)
  local copies, waits for them, and re-layouts  1.77 us (4%)
    pallas_call x1, Pallas kernels, shards(): pl.pallas_call(functools.partial(kernel, n_blk, n_bulk), out_shape=jax.Sh...  48.3 us
    unnamed x1, local copies, waits for them, and re-layouts  1.77 us

profile of v2, /device:TPU:1, one launch (start us, length us, event | category | flops | bytes accessed | tf_op | source)
XLA Modules:
  0.0 50.1 jit_solution(850393642717489403)
XLA Ops:
  0.0 48.3 %shard_map.37 = f32[1,4,96,192]{3,2,1,0:T(8,128)} custom-call(f32[1,4,96,192]{3,2,1,0:T(8,128)} %t_hbm.1, f32[1,4,96,192]{3,2,1,0:T(8,128)} %s_hbm.1, f32[4,96,192]{2,1,0:T(8,128)} %e_hbm.1), custom_call_target="tpu_custom_call" | custom-call | flops 20000000 | bytes 1200000 | tf_op jit(solution)/shard_map/pallas_call | solution.py:277
  48.3 1.8 %copy.5 = f32[1,4,96,192]{3,2,1,0:T(8,128)} copy(f32[1,4,96,192]{3,2,1,0:T(8,128)} %shard_map.37) | data formatting | bytes 589824

commit v3 on v2

--- a/solution.py
+++ b/solution.py
@@ -31,6 +31,13 @@
     return left, jnp.concatenate([low, high], axis=0)
 
 
+def each(start, count, body):
+    def step(i, carry):
+        body(start + i)
+        return carry
+    lax.fori_loop(0, count, step, 0, unroll=True)
+
+
 def ahead(cells, axis):
     return pltpu.roll(cells, cells.shape[axis] - 1, axis)
 
@@ -42,7 +49,7 @@
 def kernel(
     n_blk, n_bulk,
     t_hbm, s_hbm, e_hbm, out_ref,
-    t_in, s_in, e_in, own_s, own_t, tgt, near_s, next_s, eps, done, back, eps_wide, coef, inverse, first, mid, late, total,
+    t_in, s_in, e_in, own_s, own_t, tgt, near_s, next_s, near_rhs, next_rhs, eps, done, back, eps_wide, coef, inverse, first, mid, late, total,
     in_sem, send_sem, recv_sem,
 ):
     b, k = lax.axis_index("blk"), lax.axis_index("bulk")
@@ -81,37 +88,38 @@
         tell((swap, beside))
 
     def pack(src, dst, at):
-        def body(i, _):
+        def body(i):
             left, right = packed(src[i])
             dst[at + i, 0:lines] = left
             dst[at + i, lines:] = right
-            return 0
-        lax.fori_loop(0, SLAB, body, 0)
-
-    def copy(i, src, src_at, dst, dst_at, count, device):
+        each(0, SLAB, body)
+
+    def copy(i, src, src_at, dst, dst_at, count, device, rows=slice(None)):
         return pltpu.make_async_remote_copy(
-            src_ref=src.at[pl.ds(src_at, count)], dst_ref=dst.at[pl.ds(dst_at, count)],
+            src_ref=src.at[pl.ds(src_at, count), rows], dst_ref=dst.at[pl.ds(dst_at, count), rows],
             send_sem=send_sem.at[i], recv_sem=recv_sem.at[i], device_id=device, device_id_type=MESH,
         )
 
-    def relays(i, buf):
+    def relays(i, buf, rows=slice(None)):
         return (
-            copy(i, buf, 4 - core, buf, 7 * core, 3, mate),
-            copy(i + 1, buf, 3 + core, buf, 7 * (1 - core), 3, beyond),
+            copy(i, buf, 4 - core, buf, 7 * core, 3, mate, rows),
+            copy(i + 1, buf, 3 + core, buf, 7 * (1 - core), 3, beyond, rows),
         )
 
-    source_one = copy(0, own_s, 0, near_s, 3, SLAB, to_one)
-    source_two = copy(1, own_s, 0, next_s, 3, SLAB, to_two)
-    target = copy(2, own_t, 0, tgt, 3, SLAB, swap)
+    half = own_s.shape[1] // 2
+    parts = (slice(0, half), slice(half, 2 * half))
+
+    source_one = copy(0, own_s, 0, near_s, 0, SLAB, to_one)
+    source_two = [copy(i, own_s, 0, next_s, 0, SLAB, to_two, rows) for i, rows in zip((1, 14), parts)]
+    target = copy(2, own_t, 0, tgt, 0, SLAB, swap)
     perm = copy(3, eps, 4, eps, 4, SLAB, beside)
-    tgt_mate, tgt_beyond = relays(4, tgt)
-    near_mate, near_beyond = relays(6, near_s)
-    next_mate, next_beyond = relays(8, next_s)
-    eps_mate = copy(10, eps, 4, eps, 8 * core, SLAB, mate)
-    eps_beyond = copy(11, eps, 4, eps, 8 * (1 - core), SLAB, beyond)
+    near_mate, near_beyond = relays(4, near_rhs)
+    next_mate, next_beyond = zip(*(relays(i, next_rhs, rows) for i, rows in zip((6, 15), parts)))
+    eps_mate = copy(8, eps, 4, eps, 8 * core, SLAB, mate)
+    eps_beyond = copy(9, eps, 4, eps, 8 * (1 - core), SLAB, beyond)
 
     def result(i):
-        return copy(12 + i, done, i, back, i, 1, swap)
+        return copy(10 + i, done, i, back, i, 1, swap)
 
     loads[0].wait()
     pack(s_in, own_s, 0)
@@ -124,18 +132,17 @@
 
     @pl.when(home)
     def _():
-        pack(t_in, tgt, 3)
+        pack(t_in, tgt, 0)
         pack(e_in, eps, 4)
 
     pl.semaphore_wait(barrier, 5)
 
-    def wide_body(i, _):
+    def wide_body(i):
         left, right = unpacked(eps[i])
         eps_wide[i, :, 0:128] = left
         eps_wide[i, :, 128:WIDE] = right
-        return 0
-
-    def coef_body(i, _):
+
+    def coef_body(i):
         cells = eps_wide[i + 1]
         ahead_x = 0.5 * (cells + ahead(cells, 0))
         ahead_y = 0.5 * (cells + ahead(cells, 1))
@@ -147,42 +154,45 @@
         inverse[i] = SCALE * inv
         for j, face in enumerate((ahead_x, behind_x, ahead_y, behind_y, ahead_z, behind_z)):
             coef[j, i] = face * inv
-        return 0
+
+    def product(source, rhs, rows=slice(None)):
+        def body(i):
+            rhs[3 + i, rows] = source[i, rows] * tgt[i, rows]
+        each(0, SLAB, body)
 
     @pl.when(home)
     def _():
+        perm.start()
         source_one.start()
-        perm.start()
-        source_two.start()
         eps_mate.start()
         eps_beyond.start()
-        tgt_mate.start()
-        tgt_beyond.start()
 
     @pl.when(away)
     def _():
         target.start()
         source_one.start()
-        source_two.start()
         perm.wait_recv()
         eps_mate.start()
         eps_beyond.start()
         target.wait_recv()
-        tgt_mate.start()
-        tgt_beyond.start()
 
     source_one.wait_recv()
+    source_two[0].start()
+    source_two[1].start()
+    product(near_s, near_rhs)
     near_mate.start()
     near_beyond.start()
 
     eps_mate.wait_recv()
     eps_beyond.wait_recv()
-    lax.fori_loop(0, 12, wide_body, 0)
-    lax.fori_loop(0, 10, coef_body, 0)
-
-    source_two.wait_recv()
-    next_mate.start()
-    next_beyond.start()
+    each(0, 12, wide_body)
+    each(0, 10, coef_body)
+
+    for i, rows in enumerate(parts):
+        source_two[i].wait_recv()
+        product(next_s, next_rhs, rows)
+        next_mate[i].start()
+        next_beyond[i].start()
 
     def swept(src, i, start):
         cells = src[i]
@@ -190,38 +200,34 @@
         near = near + coef[2, start] * ahead(cells, 1) + coef[3, start] * behind(cells, 1)
         return near + coef[4, start] * src[i + 1] + coef[5, start] * src[i - 1]
 
-    def pair(source, last):
-        def first_body(i, _):
-            left, right = unpacked(source[i] * tgt[i])
+    def pair(source, rhs, last, from_mate, from_beyond):
+        def first_body(i):
+            left, right = unpacked(rhs[i])
             first[i, :, 0:128] = left * inverse[i, :, 0:128]
             first[i, :, 128:WIDE] = right * inverse[i, :, 128:WIDE]
-            return 0
-
-        lax.fori_loop(0, 10, first_body, 0)
-
-        def mid_body(i, _):
+
+        def mid_body(i):
             mid[i] = swept(first, i + 1, i + 1)
-            return 0
-
-        lax.fori_loop(0, 8, mid_body, 0)
-
-        def late_body(i, _):
+
+        def late_body(i):
             late[i] = swept(mid, i + 1, i + 2)
-            return 0
-
-        lax.fori_loop(0, 6, late_body, 0)
-
-        def out_body(i, _):
+
+        def out_body(i):
             potential = swept(late, i + 1, i + 3)
-            left, right = unpacked(source[3 + i])
+            left, right = unpacked(source[i])
             left = left * potential[:, 0:128]
             right = right * potential[:, 128:WIDE]
             if not last:
                 total[i, :, 0:128] = left
                 total[i, :, 128:WIDE] = right
-                return 0
+                return
             left = -(total[i, :, 0:128] + left)
             right = -(total[i, :, 128:WIDE] + right)
+            total[i, :, 0:128] = left
+            total[i, :, 128:WIDE] = right
+
+        def hand_over(i):
+            left, right = total[i, :, 0:128], total[i, :, 128:WIDE]
 
             @pl.when(home)
             def _():
@@ -233,20 +239,29 @@
                 done[i, 0:lines] = left
                 done[i, lines:] = jnp.concatenate([right[: lines // 2, 0:64], right[lines // 2 :, 0:64]], axis=1)
                 result(i).start()
-            return 0
-
-        lax.fori_loop(0, SLAB, out_body, 0)
-
-    tgt_mate.wait_recv()
-    tgt_beyond.wait_recv()
-    near_mate.wait_recv()
-    near_beyond.wait_recv()
-    pair(near_s, False)
-    next_mate.wait_recv()
-    next_beyond.wait_recv()
-    pair(next_s, True)
-
-    for sent in (source_one, source_two, tgt_mate, tgt_beyond, near_mate, near_beyond, next_mate, next_beyond, eps_mate, eps_beyond):
+
+        for arrival in from_mate:
+            arrival.wait_recv()
+        each(3 * (1 - core), 7, first_body)
+        each(3 * (1 - core), 5, mid_body)
+        each(3 * (1 - core), 3, late_body)
+        each(3 * (1 - core), 1, out_body)
+        if last:
+            hand_over(3 * (1 - core))
+        for arrival in from_beyond:
+            arrival.wait_recv()
+        each(7 * core, 3, first_body)
+        each(5 * core, 3, mid_body)
+        each(3 * core, 3, late_body)
+        for i in range(3):
+            out_body(core + i)
+            if last:
+                hand_over(core + i)
+
+    pair(near_s, near_rhs, False, (near_mate,), (near_beyond,))
+    pair(next_s, next_rhs, True, next_mate, next_beyond)
+
+    for sent in (source_one, *source_two, near_mate, near_beyond, *next_mate, *next_beyond, eps_mate, eps_beyond):
         sent.wait_send()
 
     @pl.when(home)
@@ -257,14 +272,14 @@
     def _():
         target.wait_send()
 
-        def back_body(i, _):
+        def back_body(i):
             result(i).wait()
             left, right = unpacked(back[i])
             out_ref[0, i, :, 0:128] = left
             out_ref[0, i, :, 128:192] = right[:, 0:64]
-            return 0
-
-        lax.fori_loop(0, SLAB, back_body, 0)
+
+        each(3 * core, 1, back_body)
+        each(1 - core, 3, back_body)
 
 
 def shards(n_blk, n_bulk, targets, sources, permittivity):
@@ -285,7 +300,9 @@
             plane_stack(planes, lines, cells),
             plane_stack(planes, rows, 128),
             plane_stack(planes, rows, 128),
-            plane_stack(10, rows, 128),
+            plane_stack(planes, rows, 128),
+            plane_stack(planes, rows, 128),
+            plane_stack(planes, rows, 128),
             plane_stack(10, rows, 128),
             plane_stack(10, rows, 128),
             plane_stack(12, rows, 128),
@@ -299,8 +316,8 @@
             plane_stack(6, lines, WIDE),
             plane_stack(planes, lines, WIDE),
             pltpu.SemaphoreType.DMA((3,)),
-            pltpu.SemaphoreType.DMA((16,)),
-            pltpu.SemaphoreType.DMA((16,)),
+            pltpu.SemaphoreType.DMA((17,)),
+            pltpu.SemaphoreType.DMA((17,)),
         ],
         compiler_params=pltpu.CompilerParams(collective_id=0, has_side_effects=True, vmem_limit_bytes=60 << 20),
         cost_estimate=pl.CostEstimate(flops=20_000_000, bytes_accessed=1_200_000, transcendentals=0),

time: 50.2 us -> 42.8 us (0.85)
  Pallas kernels: 48.3 us -> 40.5 us
    pallas_call x1, Pallas kernels: 48.3 us -> 40.5 us  [shards(): pl.pallas_call(functools.partial(kernel, n_blk, n_bulk), out_shape=jax.Sh...]
where the time goes in v3:
time: 42.8 us; the launch traced here: 42.3 us
  Pallas kernels  40.5 us (95%)
  local copies, waits for them, and re-layouts  1.77 us (4%)
    pallas_call x1, Pallas kernels, shards(): pl.pallas_call(functools.partial(kernel, n_blk, n_bulk), out_shape=jax.Sh...  40.5 us
    unnamed x1, local copies, waits for them, and re-layouts  1.77 us

profile of v3, /device:TPU:1, one launch (start us, length us, event | category | flops | bytes accessed | tf_op | source)
XLA Modules:
  0.0 42.3 jit_solution(7808329163703048180)
XLA Ops:
  0.0 40.5 %shard_map.37 = f32[1,4,96,192]{3,2,1,0:T(8,128)} custom-call(f32[1,4,96,192]{3,2,1,0:T(8,128)} %t_hbm.1, f32[1,4,96,192]{3,2,1,0:T(8,128)} %s_hbm.1, f32[4,96,192]{2,1,0:T(8,128)} %e_hbm.1), custom_call_target="tpu_custom_call" | custom-call | flops 20000000 | bytes 1200000 | tf_op jit(solution)/shard_map/pallas_call | solution.py:292
  40.5 1.8 %copy.5 = f32[1,4,96,192]{3,2,1,0:T(8,128)} copy(f32[1,4,96,192]{3,2,1,0:T(8,128)} %shard_map.37) | data formatting | bytes 589824

commit v4 on v3

--- a/solution.py
+++ b/solution.py
@@ -169,8 +169,8 @@
 
     @pl.when(away)
     def _():
+        source_one.start()
         target.start()
-        source_one.start()
         perm.wait_recv()
         eps_mate.start()
         eps_beyond.start()
@@ -184,9 +184,8 @@
     near_beyond.start()
 
     eps_mate.wait_recv()
-    eps_beyond.wait_recv()
-    each(0, 12, wide_body)
-    each(0, 10, coef_body)
+    each(4 * (1 - core), 8, wide_body)
+    each(4 * (1 - core), 6, coef_body)
 
     for i, rows in enumerate(parts):
         source_two[i].wait_recv()
@@ -194,72 +193,71 @@
         next_mate[i].start()
         next_beyond[i].start()
 
-    def swept(src, i, start):
-        cells = src[i]
-        near = first[start] + coef[0, start] * ahead(cells, 0) + coef[1, start] * behind(cells, 0)
+    def swept(j, src, i, start):
+        cells = src[j, i]
+        near = first[j, start] + coef[0, start] * ahead(cells, 0) + coef[1, start] * behind(cells, 0)
         near = near + coef[2, start] * ahead(cells, 1) + coef[3, start] * behind(cells, 1)
-        return near + coef[4, start] * src[i + 1] + coef[5, start] * src[i - 1]
-
-    def pair(source, rhs, last, from_mate, from_beyond):
-        def first_body(i):
-            left, right = unpacked(rhs[i])
-            first[i, :, 0:128] = left * inverse[i, :, 0:128]
-            first[i, :, 128:WIDE] = right * inverse[i, :, 128:WIDE]
-
-        def mid_body(i):
-            mid[i] = swept(first, i + 1, i + 1)
-
-        def late_body(i):
-            late[i] = swept(mid, i + 1, i + 2)
-
-        def out_body(i):
-            potential = swept(late, i + 1, i + 3)
-            left, right = unpacked(source[i])
-            left = left * potential[:, 0:128]
-            right = right * potential[:, 128:WIDE]
-            if not last:
-                total[i, :, 0:128] = left
-                total[i, :, 128:WIDE] = right
-                return
-            left = -(total[i, :, 0:128] + left)
-            right = -(total[i, :, 128:WIDE] + right)
-            total[i, :, 0:128] = left
-            total[i, :, 128:WIDE] = right
-
-        def hand_over(i):
-            left, right = total[i, :, 0:128], total[i, :, 128:WIDE]
-
-            @pl.when(home)
-            def _():
-                out_ref[0, i, :, 0:128] = left
-                out_ref[0, i, :, 128:192] = right[:, 0:64]
-
-            @pl.when(away)
-            def _():
-                done[i, 0:lines] = left
-                done[i, lines:] = jnp.concatenate([right[: lines // 2, 0:64], right[lines // 2 :, 0:64]], axis=1)
-                result(i).start()
-
-        for arrival in from_mate:
+        return near + coef[4, start] * src[j, i + 1] + coef[5, start] * src[j, i - 1]
+
+    def first_body(j, rhs, i):
+        left, right = unpacked(rhs[i])
+        first[j, i, :, 0:128] = left * inverse[i, :, 0:128]
+        first[j, i, :, 128:WIDE] = right * inverse[i, :, 128:WIDE]
+
+    def mid_body(j, i):
+        mid[j, i] = swept(j, first, i + 1, i + 1)
+
+    def late_body(j, i):
+        late[j, i] = swept(j, mid, i + 1, i + 2)
+
+    def weighted(j, source, i):
+        potential = swept(j, late, i + 1, i + 3)
+        left, right = unpacked(source[i])
+        return left * potential[:, 0:128], right * potential[:, 128:WIDE]
+
+    def sooner(j, rhs, arrivals):
+        for arrival in arrivals:
             arrival.wait_recv()
-        each(3 * (1 - core), 7, first_body)
-        each(3 * (1 - core), 5, mid_body)
-        each(3 * (1 - core), 3, late_body)
-        each(3 * (1 - core), 1, out_body)
-        if last:
-            hand_over(3 * (1 - core))
-        for arrival in from_beyond:
+        each(4 * (1 - core), 6, functools.partial(first_body, j, rhs))
+        each(4 * (1 - core), 4, functools.partial(mid_body, j))
+        each(4 * (1 - core), 2, functools.partial(late_body, j))
+
+    def later(j, rhs, arrivals):
+        for arrival in arrivals:
             arrival.wait_recv()
-        each(7 * core, 3, first_body)
-        each(5 * core, 3, mid_body)
-        each(3 * core, 3, late_body)
-        for i in range(3):
-            out_body(core + i)
-            if last:
-                hand_over(core + i)
-
-    pair(near_s, near_rhs, False, (near_mate,), (near_beyond,))
-    pair(next_s, next_rhs, True, next_mate, next_beyond)
+        each(6 * core, 4, functools.partial(first_body, j, rhs))
+        each(4 * core, 4, functools.partial(mid_body, j))
+        each(2 * core, 4, functools.partial(late_body, j))
+
+    def near_out(i):
+        total[i, :, 0:128], total[i, :, 128:WIDE] = weighted(0, near_s, i)
+
+    def hand_over(i):
+        left, right = weighted(1, next_s, i)
+        left = -(total[i, :, 0:128] + left)
+        right = -(total[i, :, 128:WIDE] + right)
+
+        @pl.when(home)
+        def _():
+            out_ref[0, i, :, 0:128] = left
+            out_ref[0, i, :, 128:192] = right[:, 0:64]
+
+        @pl.when(away)
+        def _():
+            done[i, 0:lines] = left
+            done[i, lines:] = jnp.concatenate([right[: lines // 2, 0:64], right[lines // 2 :, 0:64]], axis=1)
+            result(i).start()
+
+    sooner(0, near_rhs, (near_mate,))
+    sooner(1, next_rhs, next_mate)
+    eps_beyond.wait_recv()
+    each(8 * core, 4, wide_body)
+    each(6 * core, 4, coef_body)
+    later(0, near_rhs, (near_beyond,))
+    each(0, SLAB, near_out)
+    later(1, next_rhs, next_beyond)
+    for i in range(SLAB):
+        hand_over(i)
 
     for sent in (source_one, *source_two, near_mate, near_beyond, *next_mate, *next_beyond, eps_mate, eps_beyond):
         sent.wait_send()
@@ -278,8 +276,7 @@
             out_ref[0, i, :, 0:128] = left
             out_ref[0, i, :, 128:192] = right[:, 0:64]
 
-        each(3 * core, 1, back_body)
-        each(1 - core, 3, back_body)
+        each(0, SLAB, back_body)
 
 
 def shards(n_blk, n_bulk, targets, sources, permittivity):
@@ -311,9 +308,9 @@
             plane_stack(12, lines, WIDE),
             pltpu.VMEM((6, 10, lines, WIDE), jnp.float32),
             plane_stack(10, lines, WIDE),
-            plane_stack(10, lines, WIDE),
-            plane_stack(8, lines, WIDE),
-            plane_stack(6, lines, WIDE),
+            pltpu.VMEM((2, 10, lines, WIDE), jnp.float32),
+            pltpu.VMEM((2, 8, lines, WIDE), jnp.float32),
+            pltpu.VMEM((2, 6, lines, WIDE), jnp.float32),
             plane_stack(planes, lines, WIDE),
             pltpu.SemaphoreType.DMA((3,)),
             pltpu.SemaphoreType.DMA((17,)),

time: 42.8 us -> 42.5 us (level)
  no operation moved by 1% of the time
where the time goes in v4:
time: 42.5 us; the launch traced here: 42.3 us
  Pallas kernels  40.5 us (95%)
  local copies, waits for them, and re-layouts  1.77 us (4%)
    pallas_call x1, Pallas kernels, shards(): pl.pallas_call(functools.partial(kernel, n_blk, n_bulk), out_shape=jax.Sh...  40.5 us
    unnamed x1, local copies, waits for them, and re-layouts  1.77 us

profile of v4, /device:TPU:1, one launch (start us, length us, event | category | flops | bytes accessed | tf_op | source)
XLA Modules:
  0.0 42.3 jit_solution(2950204859092825963)
XLA Ops:
  0.0 40.5 %shard_map.37 = f32[1,4,96,192]{3,2,1,0:T(8,128)} custom-call(f32[1,4,96,192]{3,2,1,0:T(8,128)} %t_hbm.1, f32[1,4,96,192]{3,2,1,0:T(8,128)} %s_hbm.1, f32[4,96,192]{2,1,0:T(8,128)} %e_hbm.1), custom_call_target="tpu_custom_call" | custom-call | flops 20000000 | bytes 1200000 | tf_op jit(solution)/shard_map/pallas_call | solution.py:289
  40.6 1.8 %copy.5 = f32[1,4,96,192]{3,2,1,0:T(8,128)} copy(f32[1,4,96,192]{3,2,1,0:T(8,128)} %shard_map.37) | data formatting | bytes 589824

commit v5 on v4

--- a/solution.py
+++ b/solution.py
@@ -316,7 +316,7 @@
             pltpu.SemaphoreType.DMA((17,)),
             pltpu.SemaphoreType.DMA((17,)),
         ],
-        compiler_params=pltpu.CompilerParams(collective_id=0, has_side_effects=True, vmem_limit_bytes=60 << 20),
+        compiler_params=pltpu.CompilerParams(collective_id=0, has_side_effects=True, vmem_limit_bytes=(53 << 20) + (3 << 17)),
         cost_estimate=pl.CostEstimate(flops=20_000_000, bytes_accessed=1_200_000, transcendentals=0),
     )(targets, sources, permittivity)
 

time: 42.5 us -> 40.7 us (0.958)
  local copies, waits for them, and re-layouts: 1.77 us -> 0.75 us
  Pallas kernels: 40.5 us -> 39.8 us
    unnamed x1, local copies, waits for them, and re-layouts: 1.77 us -> 0.75 us
    pallas_call x1, Pallas kernels: 40.5 us -> 39.8 us  [shards(): pl.pallas_call(functools.partial(kernel, n_blk, n_bulk), out_shape=jax.Sh...]
where the time goes in v5:
time: 40.7 us; the launch traced here: 40.6 us
  Pallas kernels  39.8 us (98%)
  local copies, waits for them, and re-layouts  0.75 us (2%)
    pallas_call x1, Pallas kernels, shards(): pl.pallas_call(functools.partial(kernel, n_blk, n_bulk), out_shape=jax.Sh...  39.8 us

profile of v5, /device:TPU:1, one launch (start us, length us, event | category | flops | bytes accessed | tf_op | source)
XLA Modules:
  0.0 40.6 jit_solution(3910815840933856158)
XLA Ops:
  0.0 39.8 %shard_map.37 = f32[1,4,96,192]{3,2,1,0:T(8,128)S(1)} custom-call(f32[1,4,96,192]{3,2,1,0:T(8,128)} %t_hbm.1, f32[1,4,96,192]{3,2,1,0:T(8,128)} %s_hbm.1, f32[4,96,192]{2,1,0:T(8,128)} %e_hbm.1), custom_call_target="tpu_custom_call" | custom-call | flops 20000000 | bytes 1200000 | tf_op jit(solution)/shard_map/pallas_call | solution.py:289
  39.8 0.7 %copy.5 = f32[1,4,96,192]{3,2,1,0:T(8,128)} copy(f32[1,4,96,192]{3,2,1,0:T(8,128)S(1)} %shard_map.37) | data formatting | bytes 589824

commit v6 on v5

--- a/solution.py
+++ b/solution.py
@@ -54,19 +54,27 @@
 ):
     b, k = lax.axis_index("blk"), lax.axis_index("bulk")
     pos, core, z, hi = b // 2, lax.rem(b, 2), k // 2, lax.rem(k, 2)
-    n_pos = n_blk // 2
+    n_pos, n_z = n_blk // 2, n_bulk // 2
     lines = t_in.shape[1]
-    home = core == hi
-    away = core != hi
+
+    def worker(at, which, layer, side):
+        return at * 2 + 1 - side, 2 * layer + 1 - which
+
+    side, which = 1 - core, 1 - hi
+    home = side == hi
+    away = side != hi
     prev_pos, next_pos = lax.rem(pos + n_pos - 1, n_pos), lax.rem(pos + 1, n_pos)
     mate = (b + 1 - 2 * core, k)
-    beyond = (b + 1 - 2 * core, lax.rem(k + n_bulk - 2 + 4 * core, n_bulk))
+    beyond = (b + 1 - 2 * core, lax.rem(z + n_z - 1 + 2 * side, n_z) * 2 + hi)
     swap = (b + 1 - 2 * core, k + 1 - 2 * hi)
     beside = (b + 2 - 4 * lax.rem(pos, 2), k + 1 - 2 * hi)
-    to_one = (lax.rem(pos + core, n_pos) * 2 + hi, 2 * z + 1 - core)
-    to_two = (next_pos * 2 + hi, 2 * z + core)
-    from_one = (lax.rem(pos + n_pos - 1 + hi, n_pos) * 2 + 1 - hi, 2 * z + core)
-    from_two = (prev_pos * 2 + hi, 2 * z + core)
+    n_x = n_blk // 4
+    share = SLAB // n_x
+    alike = [(lax.rem(b + 4 * j, n_blk), k) for j in range(n_x)]
+    to_one = worker(lax.rem(pos + core, n_pos), 1 - core, z, hi)
+    to_two = worker(next_pos, core, z, hi)
+    from_one = (lax.rem(pos + n_pos - 1 + which, n_pos) * 2 + 1 - which, 2 * z + side)
+    from_two = (prev_pos * 2 + which, 2 * z + side)
 
     loads = [
         pltpu.make_async_copy(src, dst, in_sem.at[i])
@@ -102,8 +110,8 @@
 
     def relays(i, buf, rows=slice(None)):
         return (
-            copy(i, buf, 4 - core, buf, 7 * core, 3, mate, rows),
-            copy(i + 1, buf, 3 + core, buf, 7 * (1 - core), 3, beyond, rows),
+            copy(i, buf, 4 - side, buf, 7 * side, 3, mate, rows),
+            copy(i + 1, buf, 3 + side, buf, 7 * (1 - side), 3, beyond, rows),
         )
 
     half = own_s.shape[1] // 2
@@ -115,8 +123,8 @@
     perm = copy(3, eps, 4, eps, 4, SLAB, beside)
     near_mate, near_beyond = relays(4, near_rhs)
     next_mate, next_beyond = zip(*(relays(i, next_rhs, rows) for i, rows in zip((6, 15), parts)))
-    eps_mate = copy(8, eps, 4, eps, 8 * core, SLAB, mate)
-    eps_beyond = copy(9, eps, 4, eps, 8 * (1 - core), SLAB, beyond)
+    eps_mate = copy(8, eps, 4, eps, 8 * side, SLAB, mate)
+    eps_beyond = copy(9, eps, 4, eps, 8 * (1 - side), SLAB, beyond)
 
     def result(i):
         return copy(10 + i, done, i, back, i, 1, swap)
@@ -184,8 +192,8 @@
     near_beyond.start()
 
     eps_mate.wait_recv()
-    each(4 * (1 - core), 8, wide_body)
-    each(4 * (1 - core), 6, coef_body)
+    each(4 * (1 - side), 8, wide_body)
+    each(4 * (1 - side), 6, coef_body)
 
     for i, rows in enumerate(parts):
         source_two[i].wait_recv()
@@ -218,16 +226,16 @@
     def sooner(j, rhs, arrivals):
         for arrival in arrivals:
             arrival.wait_recv()
-        each(4 * (1 - core), 6, functools.partial(first_body, j, rhs))
-        each(4 * (1 - core), 4, functools.partial(mid_body, j))
-        each(4 * (1 - core), 2, functools.partial(late_body, j))
+        each(4 * (1 - side), 6, functools.partial(first_body, j, rhs))
+        each(4 * (1 - side), 4, functools.partial(mid_body, j))
+        each(4 * (1 - side), 2, functools.partial(late_body, j))
 
     def later(j, rhs, arrivals):
         for arrival in arrivals:
             arrival.wait_recv()
-        each(6 * core, 4, functools.partial(first_body, j, rhs))
-        each(4 * core, 4, functools.partial(mid_body, j))
-        each(2 * core, 4, functools.partial(late_body, j))
+        each(6 * side, 4, functools.partial(first_body, j, rhs))
+        each(4 * side, 4, functools.partial(mid_body, j))
+        each(2 * side, 4, functools.partial(late_body, j))
 
     def near_out(i):
         total[i, :, 0:128], total[i, :, 128:WIDE] = weighted(0, near_s, i)
@@ -251,8 +259,8 @@
     sooner(0, near_rhs, (near_mate,))
     sooner(1, next_rhs, next_mate)
     eps_beyond.wait_recv()
-    each(8 * core, 4, wide_body)
-    each(6 * core, 4, coef_body)
+    each(8 * side, 4, wide_body)
+    each(6 * side, 4, coef_body)
     later(0, near_rhs, (near_beyond,))
     each(0, SLAB, near_out)
     later(1, next_rhs, next_beyond)
@@ -313,8 +321,8 @@
             pltpu.VMEM((2, 6, lines, WIDE), jnp.float32),
             plane_stack(planes, lines, WIDE),
             pltpu.SemaphoreType.DMA((3,)),
-            pltpu.SemaphoreType.DMA((17,)),
-            pltpu.SemaphoreType.DMA((17,)),
+            pltpu.SemaphoreType.DMA((20,)),
+            pltpu.SemaphoreType.DMA((20,)),
         ],
         compiler_params=pltpu.CompilerParams(collective_id=0, has_side_effects=True, vmem_limit_bytes=(53 << 20) + (3 << 17)),
         cost_estimate=pl.CostEstimate(flops=20_000_000, bytes_accessed=1_200_000, transcendentals=0),

time: 40.7 us -> 40.5 us (level)
  the two profiles are of different devices: /device:TPU:1 before, /device:TPU:6 now
where the time goes in v6:
time: 40.5 us; the launch traced here: 40.4 us
  Pallas kernels  39.6 us (98%)
  local copies, waits for them, and re-layouts  0.75 us (2%)
    pallas_call x1, Pallas kernels, shards(): pl.pallas_call(functools.partial(kernel, n_blk, n_bulk), out_shape=jax.Sh...  39.6 us

profile of v6, /device:TPU:6, one launch (start us, length us, event | category | flops | bytes accessed | tf_op | source)
XLA Modules:
  0.0 40.4 jit_solution(12624795346588338259)
XLA Ops:
  0.0 39.6 %shard_map.37 = f32[1,4,96,192]{3,2,1,0:T(8,128)S(1)} custom-call(f32[1,4,96,192]{3,2,1,0:T(8,128)} %t_hbm.1, f32[1,4,96,192]{3,2,1,0:T(8,128)} %s_hbm.1, f32[4,96,192]{2,1,0:T(8,128)} %e_hbm.1), custom_call_target="tpu_custom_call" | custom-call | flops 20000000 | bytes 1200000 | tf_op jit(solution)/shard_map/pallas_call | solution.py:297
  39.6 0.7 %copy.5 = f32[1,4,96,192]{3,2,1,0:T(8,128)} copy(f32[1,4,96,192]{3,2,1,0:T(8,128)S(1)} %shard_map.37) | data formatting | bytes 589824

commit v7 on v6

--- a/solution.py
+++ b/solution.py
@@ -172,24 +172,24 @@
     def _():
         perm.start()
         source_one.start()
+        eps_beyond.start()
         eps_mate.start()
-        eps_beyond.start()
 
     @pl.when(away)
     def _():
         source_one.start()
         target.start()
         perm.wait_recv()
+        eps_beyond.start()
         eps_mate.start()
-        eps_beyond.start()
         target.wait_recv()
 
     source_one.wait_recv()
+    product(near_s, near_rhs)
+    near_beyond.start()
+    near_mate.start()
     source_two[0].start()
     source_two[1].start()
-    product(near_s, near_rhs)
-    near_mate.start()
-    near_beyond.start()
 
     eps_mate.wait_recv()
     each(4 * (1 - side), 8, wide_body)
@@ -198,8 +198,8 @@
     for i, rows in enumerate(parts):
         source_two[i].wait_recv()
         product(next_s, next_rhs, rows)
+        next_beyond[i].start()
         next_mate[i].start()
-        next_beyond[i].start()
 
     def swept(j, src, i, start):
         cells = src[j, i]

time: 40.5 us -> 40.5 us (level)
  no operation moved by 1% of the time
where the time goes in v7:
time: 40.5 us; the launch traced here: 40.4 us
  Pallas kernels  39.6 us (98%)
  local copies, waits for them, and re-layouts  0.75 us (2%)
    pallas_call x1, Pallas kernels, shards(): pl.pallas_call(functools.partial(kernel, n_blk, n_bulk), out_shape=jax.Sh...  39.6 us

profile of v7, /device:TPU:6, one launch (start us, length us, event | category | flops | bytes accessed | tf_op | source)
XLA Modules:
  0.0 40.4 jit_solution(1056593773187881102)
XLA Ops:
  0.0 39.6 %shard_map.37 = f32[1,4,96,192]{3,2,1,0:T(8,128)S(1)} custom-call(f32[1,4,96,192]{3,2,1,0:T(8,128)} %t_hbm.1, f32[1,4,96,192]{3,2,1,0:T(8,128)} %s_hbm.1, f32[4,96,192]{2,1,0:T(8,128)} %e_hbm.1), custom_call_target="tpu_custom_call" | custom-call | flops 20000000 | bytes 1200000 | tf_op jit(solution)/shard_map/pallas_call | solution.py:297
  39.6 0.7 %copy.5 = f32[1,4,96,192]{3,2,1,0:T(8,128)} copy(f32[1,4,96,192]{3,2,1,0:T(8,128)S(1)} %shard_map.37) | data formatting | bytes 589824

commit v8 on v7

--- a/solution.py
+++ b/solution.py
@@ -117,11 +117,11 @@
     half = own_s.shape[1] // 2
     parts = (slice(0, half), slice(half, 2 * half))
 
-    source_one = copy(0, own_s, 0, near_s, 0, SLAB, to_one)
+    source_one = [copy(i, own_s, 0, near_s, 0, SLAB, to_one, rows) for i, rows in zip((0, 17), parts)]
     source_two = [copy(i, own_s, 0, next_s, 0, SLAB, to_two, rows) for i, rows in zip((1, 14), parts)]
     target = copy(2, own_t, 0, tgt, 0, SLAB, swap)
     perm = copy(3, eps, 4, eps, 4, SLAB, beside)
-    near_mate, near_beyond = relays(4, near_rhs)
+    near_mate, near_beyond = zip(*(relays(i, near_rhs, rows) for i, rows in zip((4, 18), parts)))
     next_mate, next_beyond = zip(*(relays(i, next_rhs, rows) for i, rows in zip((6, 15), parts)))
     eps_mate = copy(8, eps, 4, eps, 8 * side, SLAB, mate)
     eps_beyond = copy(9, eps, 4, eps, 8 * (1 - side), SLAB, beyond)
@@ -171,25 +171,27 @@
     @pl.when(home)
     def _():
         perm.start()
-        source_one.start()
+        source_one[0].start()
+        source_one[1].start()
         eps_beyond.start()
         eps_mate.start()
 
     @pl.when(away)
     def _():
-        source_one.start()
+        source_one[0].start()
+        source_one[1].start()
         target.start()
         perm.wait_recv()
         eps_beyond.start()
         eps_mate.start()
         target.wait_recv()
 
-    source_one.wait_recv()
-    product(near_s, near_rhs)
-    near_beyond.start()
-    near_mate.start()
-    source_two[0].start()
-    source_two[1].start()
+    for i, rows in enumerate(parts):
+        source_one[i].wait_recv()
+        product(near_s, near_rhs, rows)
+        near_beyond[i].start()
+        near_mate[i].start()
+        source_two[i].start()
 
     eps_mate.wait_recv()
     each(4 * (1 - side), 8, wide_body)
@@ -256,18 +258,18 @@
             done[i, lines:] = jnp.concatenate([right[: lines // 2, 0:64], right[lines // 2 :, 0:64]], axis=1)
             result(i).start()
 
-    sooner(0, near_rhs, (near_mate,))
+    sooner(0, near_rhs, near_mate)
     sooner(1, next_rhs, next_mate)
     eps_beyond.wait_recv()
     each(8 * side, 4, wide_body)
     each(6 * side, 4, coef_body)
-    later(0, near_rhs, (near_beyond,))
+    later(0, near_rhs, near_beyond)
     each(0, SLAB, near_out)
     later(1, next_rhs, next_beyond)
     for i in range(SLAB):
         hand_over(i)
 
-    for sent in (source_one, *source_two, near_mate, near_beyond, *next_mate, *next_beyond, eps_mate, eps_beyond):
+    for sent in (*source_one, *source_two, *near_mate, *near_beyond, *next_mate, *next_beyond, eps_mate, eps_beyond):
         sent.wait_send()
 
     @pl.when(home)

time: 40.5 us -> 41.2 us (1.017)
  Pallas kernels: 39.6 us -> 40.3 us
    pallas_call x1, Pallas kernels: 39.6 us -> 40.3 us  [shards(): pl.pallas_call(functools.partial(kernel, n_blk, n_bulk), out_shape=jax.Sh...]
where the time goes in v8:
time: 41.2 us; the launch traced here: 41 us
  Pallas kernels  40.3 us (98%)
  local copies, waits for them, and re-layouts  0.75 us (2%)
    pallas_call x1, Pallas kernels, shards(): pl.pallas_call(functools.partial(kernel, n_blk, n_bulk), out_shape=jax.Sh...  40.3 us

profile of v8, /device:TPU:6, one launch (start us, length us, event | category | flops | bytes accessed | tf_op | source)
XLA Modules:
  0.0 41.0 jit_solution(2154135366486387593)
XLA Ops:
  0.0 40.3 %shard_map.37 = f32[1,4,96,192]{3,2,1,0:T(8,128)S(1)} custom-call(f32[1,4,96,192]{3,2,1,0:T(8,128)} %t_hbm.1, f32[1,4,96,192]{3,2,1,0:T(8,128)} %s_hbm.1, f32[4,96,192]{2,1,0:T(8,128)} %e_hbm.1), custom_call_target="tpu_custom_call" | custom-call | flops 20000000 | bytes 1200000 | tf_op jit(solution)/shard_map/pallas_call | solution.py:299
  40.3 0.7 %copy.5 = f32[1,4,96,192]{3,2,1,0:T(8,128)} copy(f32[1,4,96,192]{3,2,1,0:T(8,128)S(1)} %shard_map.37) | data formatting | bytes 589824
